TPU v7x, 256 devices: a whole 4x4x8 slice. The times are simulated.
256 devices in a mesh: attn: 8 (over z_hi, core), ffn: 8 (over z_lo, x), tp: 4 (over y).
Axes of the slice: x: 4, y: 4, z: 8 (z_hi: 4, z_lo: 2; z = z_hi * 2 + z_lo), core: 2. Of those that a mesh axis runs over, the one named last changes fastest.
Arguments:
- queries: bfloat16 [2048, 4096], P(('attn', 'ffn'), 'tp'), may hold values from -4.5 to 4.5
- keys: bfloat16 [2048, 128, 512], P(('attn', 'ffn'), None, 'tp'), may hold values from -4.5 to 4.5
- values: bfloat16 [2048, 128, 512], P(('attn', 'ffn'), None, 'tp'), may hold values from -4.5 to 4.5
- lengths: int32 [2048], P(('attn', 'ffn')), may hold values from 0 to 128, as said below
- routes: int32 [2048, 1], P(('attn', 'ffn')), may hold values from 0 to 7; in each aligned block of 32 rows (0 to 31, 32 to 63, ...) at most 8 rows name the same one
- residual: bfloat16 [2048, 4096], P(('attn', 'ffn')), may hold values from -20 to 20
- w_out: bfloat16 [4096, 4096], P(None, ('attn', 'tp')), may hold values from -0.09375 to 0.09375
- norm_gain: float32 [4096], P(('attn', 'tp')), may hold values from 0.1 to 1.9
- w_gate: bfloat16 [8, 4096, 14336], P('ffn', None, ('attn', 'tp')), may hold values from -0.09375 to 0.09375
- w_up: bfloat16 [8, 4096, 14336], P('ffn', None, ('attn', 'tp')), may hold values from -0.09375 to 0.09375
- w_down: bfloat16 [8, 14336, 4096], P('ffn', ('attn', 'tp')), may hold values from -0.09375 to 0.09375
Outputs:
- stream: bfloat16 [2048, 4096], P(('attn', 'ffn'))
- group_sums: float32 [8, 4096], P('ffn', ('attn', 'tp'))
Inputs may be any that keep to these rules, and one draw needn't show every extreme that they name: `lengths`: 0 marks an empty slot, else the number of cached positions of its candidate. `routes`: in each aligned block of 32 rows no group is named by more than 8 rows.
All inputs are finite; a program needn't handle non-finite values.
Results may differ from a plain program's by a relative error of at most 0.018.
Values may be sent and summed in bfloat16 or wider, within the bound.
A program may use at most 128 MiB of HBM per device.

v0:
```python
import math

import jax
import jax.numpy as jnp
from jax import lax
from jax.sharding import PartitionSpec as P

QH = 32
KVH = 4
HD = 128


EPSILON = 1e-05


def attend(queries, keys, values, lengths):
    slot_count = queries.shape[0]
    length = keys.shape[1]
    local_kv = keys.shape[2] // HD
    group_size = QH // KVH
    query_heads = queries.reshape(slot_count, local_kv, group_size, HD)
    key_heads = keys.reshape(slot_count, length, local_kv, HD)
    value_heads = values.reshape(slot_count, length, local_kv, HD)
    scores = jnp.einsum(
        "skgd,slkd->skgl", query_heads, key_heads, preferred_element_type=jnp.float32
    ) / math.sqrt(HD)
    valid = lax.broadcasted_iota(jnp.int32, (slot_count, length), 1) < lengths[:, None]
    valid_mask = valid[:, None, None, :]
    row_max = jnp.max(jnp.where(valid_mask, scores, -1e30), axis=-1, keepdims=True)
    unnormed = jnp.where(valid_mask, jnp.exp(scores - row_max), 0.0)
    summed = jnp.maximum(jnp.sum(unnormed, axis=-1, keepdims=True), 1.0)
    weights = (unnormed / summed).astype(jnp.bfloat16)
    combined = jnp.einsum(
        "skgl,slkd->skgd", weights, value_heads, preferred_element_type=jnp.float32
    )
    return combined.reshape(slot_count, -1).astype(jnp.bfloat16)


def place_rows(placing, source):
    return jnp.dot(placing, source, preferred_element_type=jnp.float32).astype(jnp.bfloat16)


def per_device(
    queries, keys, values, lengths, routes, residual, w_out, norm_gain, w_gate, w_up, w_down
):
    attn_size = lax.axis_size("attn")
    ffn_size = lax.axis_size("ffn")
    tp_size = lax.axis_size("tp")
    tp_index = lax.axis_index("tp")
    slot_count = queries.shape[0]
    model_width = residual.shape[1]
    block_width = w_out.shape[1]
    capacity = max(2, 2 * slot_count // ffn_size)
    buffer_rows = ffn_size * capacity
    gate_weights = w_gate[0]
    up_weights = w_up[0]
    down_weights = w_down[0]
    occupied = lengths > 0
    destination = routes[:, 0]
    earlier = lax.broadcasted_iota(jnp.int32, (slot_count, slot_count), 1) < lax.broadcasted_iota(
        jnp.int32, (slot_count, slot_count), 0
    )
    same_group = (destination[:, None] == destination[None, :]) & occupied[None, :] & earlier
    rank_in_group = jnp.sum(same_group.astype(jnp.int32), axis=1)
    target = destination * capacity + rank_in_group
    placing = (
        lax.broadcasted_iota(jnp.int32, (buffer_rows, slot_count), 0) == target[None, :]
    ) & occupied[None, :]
    placing = placing.astype(jnp.bfloat16)
    picked = residual.reshape(slot_count, attn_size, tp_size, block_width)
    picked = lax.dynamic_index_in_dim(picked, tp_index, 2, keepdims=False).reshape(
        slot_count, attn_size * block_width
    )
    send_x = place_rows(placing, picked)
    attended = attend(queries, keys, values, lengths)
    send_o = place_rows(placing, attended)
    recv_o, recv_x = (
        lax.all_to_all(send_o, "ffn", split_axis=0, concat_axis=0, tiled=True),
        lax.all_to_all(send_x, "ffn", split_axis=0, concat_axis=0, tiled=True),
    )
    cols_x = lax.all_to_all(recv_x, "attn", split_axis=1, concat_axis=0, tiled=True)
    heads_all = lax.all_gather(recv_o, "tp", axis=1, tiled=True)
    projected = jnp.dot(
        lax.all_gather(heads_all, "attn", axis=0, tiled=True),
        w_out,
        preferred_element_type=jnp.float32,
    )
    hidden = cols_x.astype(jnp.float32) + projected
    squares = lax.psum(jnp.sum(hidden * hidden, axis=1), ("attn", "tp"))
    inverse_rms = lax.rsqrt(squares / model_width + EPSILON)
    normed = (hidden * inverse_rms[:, None] * norm_gain[None, :]).astype(jnp.bfloat16)
    shard_cols = lax.all_gather(normed, ("attn", "tp"), axis=1, tiled=True)
    gate_sum = jnp.dot(shard_cols, gate_weights, preferred_element_type=jnp.float32)
    up_sum = jnp.dot(shard_cols, up_weights, preferred_element_type=jnp.float32)
    activated = (jax.nn.silu(gate_sum) * up_sum).astype(jnp.bfloat16)
    partial_down = jnp.dot(activated, down_weights, preferred_element_type=jnp.float32)
    down_here = lax.psum_scatter(
        partial_down.astype(jnp.bfloat16), ("attn", "tp"), scatter_dimension=1, tiled=True
    ).astype(jnp.float32)
    result = (hidden + down_here).astype(jnp.bfloat16)
    group_part = jnp.sum(down_here, axis=0)[None, :]
    swapped = lax.all_to_all(result, "attn", split_axis=0, concat_axis=1, tiled=True)
    assembled = lax.all_gather(
        swapped.reshape(buffer_rows, attn_size, 1, block_width), "tp", axis=2, tiled=True
    )
    assembled = lax.all_to_all(assembled, "ffn", split_axis=0, concat_axis=0, tiled=True)
    returned = assembled.reshape(buffer_rows, model_width)
    stream = lax.dot_general(
        placing, returned, (((0,), (0,)), ((), ())), preferred_element_type=jnp.float32
    ).astype(jnp.bfloat16)
    return (stream, group_part)


def solution(mesh):
    placed = (
        P(("attn", "ffn"), "tp"),
        P(("attn", "ffn"), None, "tp"),
        P(("attn", "ffn"), None, "tp"),
        P(("attn", "ffn")),
        P(("attn", "ffn"), None),
        P(("attn", "ffn"), None),
        P(None, ("attn", "tp")),
        P(("attn", "tp")),
        P("ffn", None, ("attn", "tp")),
        P("ffn", None, ("attn", "tp")),
        P("ffn", ("attn", "tp"), None),
    )
    return jax.shard_map(
        per_device,
        mesh=mesh,
        in_specs=placed,
        out_specs=(P(("attn", "ffn"), None), P("ffn", ("attn", "tp"))),
        check_vma=False,
    )
```

profile of v0, /device:TPU:1, one launch (start us, length us, event | category | flops | bytes accessed | tf_op | source)
XLA Modules:
  0.0 408.0 jit_solution(15468320191585917852)
XLA Ops:
  7.2 0.0 copy-start
  7.2 0.0 copy-start.1
  7.2 0.0 all-gather.4.cloned.1.call-start
  7.2 0.8 broadcast_compare_fusion
  8.0 0.7 iota_compare_fusion.1
  8.7 0.9 convert_reduce_fusion.1
  9.6 0.7 multiply_add_fusion
  10.3 0.8 copy.29
  11.2 1.9 convolution_multiply_fusion
  13.0 5.3 %fusion.38 = (f32[32,8]{1,0:T(8,128)S(1)}, f32[32,8,128]{2,1,0:T(8,128)S(1)}) fusion(f32[32,8,128]{2,1,0:T(8,128)S(1)} %convolution_multiply_fusion, pred[32,128]{1,0:T(8,128)(4,1)S(1)} %iota_compare_fusion.1), kind=kOutput, calls=%fused_computation.53 | output fusion | flops 131199 | bytes 267264 | tf_op jit(solution)/shard_map/sub | solution.py:30
  18.3 1.7 convolution_convert_fusion.4
  20.1 0.2 fusion.16
  20.2 11.4 %all_to_all.55 = bf16[8,8,1024]{2,1,0:T(8,128)(2,1)S(1)} all-to-all(bf16[8,8,1024]{2,1,0:T(8,128)(2,1)S(1)} %fusion.16), channel_id=1, replica_groups=mesh['attn'=8,'ffn'=8,'tp'=4] {'ffn'}, dimensions={0} | all-to-all | bytes 262144 | tf_op jit(solution)/shard_map/all_to_all | solution.py:78
  31.7 11.6 %all_gather.12 = bf16[64,4096]{1,0:T(8,128)(2,1)} all-gather(bf16[64,1024]{1,0:T(8,128)(2,1)S(1)} %bitcast.63), channel_id=1, replica_groups=mesh['attn'=8,'ffn'=8,'tp'=4] {'tp'}, dimensions={1}, use_global_device_ids=true | all-gather | bytes 655360 | tf_op jit(solution)/shard_map/all_gather | solution.py:82
  43.3 0.0 all-gather.4.cloned.1.call-update
  43.3 0.0 copy-start.2
  43.3 0.0 all-gather.6.cloned.1.call-start
  43.3 0.0 copy-done.1
  43.4 0.2 reshape.99
  43.5 0.4 dynamic-slice_reduce_fusion
  43.9 0.2 fusion.15
  44.1 8.0 %all_to_all.56 = bf16[8,8,1024]{2,1,0:T(8,128)(2,1)S(1)} all-to-all(bf16[8,8,1024]{2,1,0:T(8,128)(2,1)S(1)} %fusion.15), channel_id=1, replica_groups=mesh['attn'=8,'ffn'=8,'tp'=4] {'ffn'}, dimensions={0} | all-to-all | bytes 262144 | tf_op jit(solution)/shard_map/all_to_all | solution.py:79
  52.1 25.2 %all_to_all.57 = bf16[64,8,128]{2,0,1:T(8,128)(2,1)S(1)} all-to-all(bf16[64,8,128]{2,0,1:T(8,128)(2,1)S(1)} %copy.21), channel_id=1, replica_groups=mesh['attn'=8,'ffn'=8,'tp'=4] {'attn'}, dimensions={1} | all-to-all | bytes 262144 | tf_op jit(solution)/shard_map/all_to_all | solution.py:81
  77.4 23.2 %all-gather.4.cloned.1.call-done = bf16[512,4096]{1,0:T(8,128)(2,1)} async-done(((bf16[64,4096]{1,0:T(8,128)(2,1)}), bf16[512,4096]{1,0:T(8,128)(2,1)}) %all-gather.4.cloned.1.call-update) | async-done | bytes 4194320 | tf_op jit(solution)/shard_map/all_gather | solution.py:84
  100.6 0.0 copy-done
  100.6 3.5 multiply_reduce_fusion
  104.1 70.1 %psum.7 = f32[512]{0:T(512)S(1)} all-reduce(f32[512]{0:T(512)S(1)} %get-tuple-element.6), channel_id=1, replica_groups=mesh['attn'=8,'ffn'=8,'tp'=4] {'attn','tp'}, use_global_device_ids=true, to_apply=%region_4.5 | all-reduce | flops 512 | bytes 4096 | tf_op jit(solution)/shard_map/psum | solution.py:89
  174.2 0.0 copy-done.2
  174.2 0.8 multiply_convert_fusion
  175.0 0.0 all-gather.6.cloned.1.call-update
  175.0 0.0 reduce-scatter.4.cloned.1.call-start
  175.1 67.9 %all-gather.6.cloned.1.call-done = bf16[512,4096]{1,0:T(8,128)(2,1)} async-done(((bf16[512,128]{1,0:T(8,128)(2,1)}), bf16[512,4096]{1,0:T(8,128)(2,1)}) %all-gather.6.cloned.1.call-update) | async-done | bytes 4194320 | tf_op jit(solution)/shard_map/all_gather | solution.py:92
  243.0 5.4 %fusion.4 = f32[512,448]{0,1:T(8,128)S(1)} fusion(bf16[512,4096]{1,0:T(8,128)(2,1)} %all-gather.6.cloned.1.call-done, bf16[1,4096,448]{1,2,0:T(8,128)(2,1)} %param.19), kind=kOutput, calls=%fused_computation.6 | convolution fusion | flops 1879048192 | bytes 8781824 | tf_op jit(solution)/shard_map/dot_general | solution.py:93
  248.4 10.7 %convolution_convert_fusion = bf16[512,4096]{1,0:T(8,128)(2,1)} fusion(bf16[1,448,4096]{2,1,0:T(8,128)(2,1)} %param.21, bf16[512,4096]{1,0:T(8,128)(2,1)} %all-gather.6.cloned.1.call-done, bf16[1,4096,448]{1,2,0:T(8,128)(2,1)} %param.20, f32[512,448]{0,1:T(8,128)S(1)} %fusion.4), kind=kOutput, calls=%fused_computation.1 | convolution fusion | flops 3761569792 | bytes 16646144 | tf_op jit(solution)/shard_map/dot_general | solution.py:96
  259.2 6.5 %copy.24 = bf16[512,4096]{0,1:T(8,128)(2,1)} copy(bf16[512,4096]{1,0:T(8,128)(2,1)} %convolution_convert_fusion) | data formatting | bytes 8388608
  265.7 0.0 reduce-scatter.4.cloned.1.call-update
  265.7 95.0 %reduce-scatter.4.cloned.1.call-done = bf16[128,512]{1,0:T(8,128)(2,1)} async-done(((bf16[4096,512]{1,0:T(8,128)(2,1)}), bf16[128,512]{1,0:T(8,128)(2,1)}) %reduce-scatter.4.cloned.1.call-update) | async-done | bytes 131088
  360.8 1.0 copy.25
  361.8 0.6 convert_reduce_fusion
  362.4 14.7 %all_to_all.58 = bf16[8,64,128]{2,1,0:T(8,128)(2,1)S(1)} all-to-all(bf16[8,64,128]{2,1,0:T(8,128)(2,1)S(1)} %bitcast.62), channel_id=1, replica_groups=mesh['attn'=8,'ffn'=8,'tp'=4] {'attn'}, dimensions={0} | all-to-all | bytes 262144 | tf_op jit(solution)/shard_map/all_to_all | solution.py:102
  377.1 11.6 %all-gather = bf16[64,8,512]{2,0,1:T(8,128)(2,1)S(1)} all-gather(bf16[64,8,128]{2,0,1:T(8,128)(2,1)S(1)} %bitcast.64), channel_id=2, replica_groups=mesh['attn'=8,'ffn'=8,'tp'=4] {'tp'}, dimensions={2}, use_global_device_ids=true | all-gather | bytes 655360 | tf_op jit(solution)/shard_map/all_gather | solution.py:103
  388.7 0.1 reshape.106
  388.9 0.2 copy.23
  389.1 11.0 %all_to_all.59 = bf16[64,8,4,128]{3,2,1,0:T(4,128)(2,1)S(1)} all-to-all(bf16[64,8,4,128]{3,2,1,0:T(4,128)(2,1)S(1)} %copy.23), channel_id=1, replica_groups=mesh['attn'=8,'ffn'=8,'tp'=4] {'ffn'}, dimensions={0} | all-to-all | bytes 1048576 | tf_op jit(solution)/shard_map/all_to_all | solution.py:106
  400.1 0.4 reshape.103
  400.5 1.0 convolution_convert_fusion.1
  (5 shorter events, 0.1 us)
Async XLA Ops:
  7.2 93.4 %copy-start = (bf16[4096,128]{1,0:T(8,128)(2,1)S(1)}, bf16[4096,128]{1,0:T(8,128)(2,1)}, u32[]{:S(2)}) copy-start(bf16[4096,128]{1,0:T(8,128)(2,1)} %param.17) | copy-start | bytes 3145732
  7.2 36.2 %copy-start.1 = (bf16[32,4096]{1,0:T(8,128)(2,1)S(1)}, bf16[32,4096]{1,0:T(8,128)(2,1)}, u32[]{:S(2)}) copy-start(bf16[32,4096]{1,0:T(8,128)(2,1)} %param.16) | copy-start | bytes 786436
  7.2 93.4 %all-gather.4.cloned.1.call-start = ((), (), s32[]{:S(2)}) async-start(), calls=%async_computation.6 | async-start | bytes 4718592 | tf_op jit(solution)/shard_map/all_gather | solution.py:84
  43.3 130.9 %copy-start.2 = (f32[128]{0:T(128)S(1)}, f32[128]{0:T(128)}, u32[]{:S(2)}) copy-start(f32[128]{0:T(128)} %param.18) | copy-start | bytes 1540
  43.3 199.7 %all-gather.6.cloned.1.call-start = ((), (), s32[]{:S(2)}) async-start(), calls=%async_computation.7 | async-start | bytes 4325376 | tf_op jit(solution)/shard_map/all_gather | solution.py:92
  175.0 185.7 %reduce-scatter.4.cloned.1.call-start = ((), (), s32[]{:S(2)}) async-start(), calls=%async_computation.8 | async-start | bytes 4325376
Sparse Core Ops, SparseCore 0:
  43.4 57.1 all-gather.3
  175.2 67.8 all-gather.5
  265.8 94.8 reduce-scatter.3
where the time goes:
time: 412 us; the launch traced here: 408 us
  waiting for transfers between devices  186 us (45%)
  blocking collectives  164 us (40%)
  matrix products  24.6 us (6%)
  between operations  13.9 us (3%)
  other arithmetic  9.78 us (2%)
  local copies, waits for them, and re-layouts  9.72 us (2%)
    unnamed x4, waiting for transfers between devices  95.1 us
    psum x1, blocking collectives, per_device(): squares = lax.psum(jnp.sum(hidden * hidden, axis=1), ('attn', 'tp'))  70.1 us
    all_gather x1, waiting for transfers between devices, per_device(): shard_cols = lax.all_gather(normed, ('attn', 'tp'), axis=1, tiled=True)  67.9 us
    all_to_all x1, blocking collectives, per_device(): lax.all_to_all(recv_x, 'attn', split_axis=1, concat_axis=0, tiled=True)  25.2 us
    all_gather x1, waiting for transfers between devices, per_device(): lax.all_gather(heads_all, 'attn', axis=0, tiled=True)  23.2 us
    all_to_all x1, blocking collectives, per_device(): lax.all_to_all(result, 'attn', split_axis=0, concat_axis=1, tiled=True)  14.7 us
    all_gather x1, blocking collectives, per_device(): lax.all_gather(swapped.reshape(buffer_rows, attn_size, 1, block_width), '...  11.6 us
    all_gather x1, blocking collectives, per_device(): heads_all = lax.all_gather(recv_o, 'tp', axis=1, tiled=True)  11.6 us
  transfers between devices with their start and end apart: 3, of which 3 were waited for; matrix products, arithmetic and copies ran while one was open for 0% of the time, Pallas kernels for 0%

commit v1 on v0

v1 whole, which is shorter than its diff:
```python
import functools
import math

import jax
import jax.numpy as jnp
from jax import lax
from jax.experimental import pallas as pl
from jax.experimental.pallas import tpu as pltpu
from jax.sharding import PartitionSpec as P

HD = 128
EPSILON = 1e-05
MESH = pl.DeviceIdType.MESH
BF = jnp.bfloat16
F32 = jnp.float32
Z_ORDER = (1, 3, 2)
RS_ORDER = (2, 1, 3, 0)


def iota(shape, dim):
    return lax.broadcasted_iota(jnp.int32, shape, dim)


def position():
    return lax.axis_index("attn"), lax.axis_index("ffn"), lax.axis_index("tp")


def remote(src, dst, send, recv, device):
    return pltpu.make_async_remote_copy(
        src_ref=src, dst_ref=dst, send_sem=send, recv_sem=recv, device_id=device, device_id_type=MESH
    )


def greet(devices):
    barrier = pltpu.get_barrier_semaphore()
    for device in devices:
        pl.semaphore_signal(barrier, inc=1, device_id=device, device_id_type=MESH)
    return lambda: pl.semaphore_wait(barrier, len(devices))


def gather_group(buf, half, zs, zr, ys, yr, hs, hr, cs, cr, consume):
    a, f, t = position()
    right, left = lax.rem(t + 1, 4), lax.rem(t + 3, 4)
    opposite = lax.rem(t + 2, 4)
    sibling = a + 1 - 2 * lax.rem(a, 2)
    rows = buf.shape[2]
    first, second = pl.ds(0, half), pl.ds(half, rows - half)
    source = [a] + [lax.rem(a + 8 - 2 * dz, 8) for dz in Z_ORDER]
    sent = []

    def start(copy):
        copy.start()
        sent.append(copy)

    def z_send(k):
        start(remote(buf.at[a, t], buf.at[a, t], zs.at[k], zr.at[k], (lax.rem(a + 2 * Z_ORDER[k], 8), f, t)))

    def z_wait(k):
        slot = buf.at[source[k + 1], t]
        remote(slot, slot, zs.at[k], zr.at[k], (a, f, right)).wait_recv()

    def y_send(k):
        slot = buf.at[source[k], t]
        start(remote(slot, slot, ys.at[k, 0], yr.at[k, 0], (a, f, right)))
        start(remote(slot, slot, ys.at[k, 1], yr.at[k, 1], (a, f, left)))

    def y_forward(k):
        slot = buf.at[source[k], left]
        remote(slot, slot, ys.at[k, 0], yr.at[k, 0], (a, f, right)).wait_recv()
        piece = slot.at[first]
        start(remote(piece, piece, hs.at[k, 0], hr.at[k, 0], (a, f, right)))
        slot = buf.at[source[k], right]
        remote(slot, slot, ys.at[k, 1], yr.at[k, 1], (a, f, left)).wait_recv()
        piece = slot.at[second]
        start(remote(piece, piece, hs.at[k, 1], hr.at[k, 1], (a, f, left)))

    def core_send(k):
        slot = buf.at[source[k], opposite]
        remote(slot.at[first], slot.at[first], hs.at[k, 0], hr.at[k, 0], (a, f, right)).wait_recv()
        remote(slot.at[second], slot.at[second], hs.at[k, 1], hr.at[k, 1], (a, f, left)).wait_recv()
        chunk = buf.at[source[k]]
        start(remote(chunk, chunk, cs.at[k], cr.at[k], (sibling, f, t)))

    def core_wait(k):
        other = source[k] + 1 - 2 * lax.rem(a, 2)
        chunk = buf.at[other]
        remote(chunk, chunk, cs.at[k], cr.at[k], (sibling, f, t)).wait_recv()
        consume(lax.div(source[k], 2))

    for k in range(3):
        z_send(k)
    y_send(0)
    z_wait(0)
    y_send(1)
    y_forward(0)
    z_wait(1)
    y_send(2)
    y_forward(1)
    core_send(0)
    z_wait(2)
    y_send(3)
    y_forward(2)
    core_send(1)
    core_wait(0)
    y_forward(3)
    core_send(2)
    core_wait(1)
    core_send(3)
    core_wait(2)
    core_wait(3)
    return sent


GATHER_SEMS = [
    pltpu.SemaphoreType.DMA((3,)),
    pltpu.SemaphoreType.DMA((3,)),
    pltpu.SemaphoreType.DMA((4, 2)),
    pltpu.SemaphoreType.DMA((4, 2)),
    pltpu.SemaphoreType.DMA((4, 2)),
    pltpu.SemaphoreType.DMA((4, 2)),
    pltpu.SemaphoreType.DMA((4,)),
    pltpu.SemaphoreType.DMA((4,)),
]


def attend(q, k, v, lens, att):
    for part in range(2):
        base = part * 16
        heads = jnp.concatenate([q[base : base + 16, h * HD : (h + 1) * HD] for h in range(8)], axis=0)
        slot = lax.rem(iota((128, 128), 0), 16)
        scores = jnp.zeros((128, 128), F32)
        for pair in range(8):
            block = k[base + 2 * pair : base + 2 * pair + 2].reshape(256, HD)
            both = lax.dot_general(heads, block, (((1,), (1,)), ((), ())), preferred_element_type=F32)
            scores = jnp.where(slot == 2 * pair, both[:, :128], scores)
            scores = jnp.where(slot == 2 * pair + 1, both[:, 128:], scores)
        scores = scores / math.sqrt(HD)
        limit = jnp.concatenate([lens[base : base + 16, :]] * 8, axis=0)
        valid = iota((128, 128), 1) < limit
        top = jnp.max(jnp.where(valid, scores, -1e30), axis=-1, keepdims=True)
        unnormed = jnp.where(valid, jnp.exp(scores - top), 0.0)
        summed = jnp.maximum(jnp.sum(unnormed, axis=-1, keepdims=True), 1.0)
        weights = unnormed / summed
        total = jnp.zeros((128, HD), F32)
        for pair in range(8):
            block = v[base + 2 * pair : base + 2 * pair + 2].reshape(256, HD)
            masked = jnp.concatenate(
                [jnp.where(slot == 2 * pair, weights, 0.0), jnp.where(slot == 2 * pair + 1, weights, 0.0)], axis=1
            ).astype(BF)
            total = total + jnp.dot(masked, block, preferred_element_type=F32)
        total = total.astype(BF)
        for h in range(8):
            att[pl.ds(base, 16), pl.ds(h * HD, HD)] = total[h * 16 : (h + 1) * 16, :]


def project_kernel(
    q_hbm, k_hbm, v_hbm, lens, codes, res_hbm, wout_hbm,
    h_out, hidden, back_out, table_out, need_out,
    q, k, v, wout, buf, res, cbuf, place, sbuf, hbuf, tsend, tbuf,
    in_sems, rs, rr, es, er, fs, fr, gs, gr, own_sem, *gather_sems,
):
    a, f, t = position()
    loads = []
    for i, (src, dst) in enumerate(((q_hbm, q), (k_hbm, k), (v_hbm, v), (wout_hbm, wout))):
        copy = pltpu.make_async_copy(src, dst, in_sems.at[i])
        copy.start()
        loads.append(copy)
    attn_peers = [lax.rem(a + step, 8) for step in range(1, 8)]
    ffn_peers = [lax.rem(f + step, 8) for step in range(1, 8)]
    all_here = greet(
        [(peer, f, t) for peer in attn_peers]
        + [(a, peer, t) for peer in ffn_peers]
        + [(a, f, lax.rem(t + 1, 4)), (a, f, lax.rem(t + 3, 4))]
    )
    all_here()

    def columns(index):
        return pl.ds(pl.multiple_of((index * 4 + t) * HD, HD), HD)

    sent = []
    cbuf[a] = codes[...]
    for i, peer in enumerate(attn_peers):
        copy = remote(res_hbm.at[:, columns(peer)], res.at[a], rs.at[i], rr.at[i], (peer, f, t))
        copy.start()
        sent.append(copy)
        copy = remote(codes, cbuf.at[a], es.at[i], er.at[i], (peer, f, t))
        copy.start()
        sent.append(copy)
    own = pltpu.make_async_copy(res_hbm.at[:, columns(a)], res.at[a], own_sem)
    own.start()
    for copy in loads[:3]:
        copy.wait()
    attend(q, k, v, lens, buf.at[a, t])

    def consume(z):
        pair = pl.ds(2 * z, 2)
        total = jnp.zeros((64, HD), F32)
        for other in range(4):
            left = buf[pair, other].reshape(64, 1024)
            total = total + jnp.dot(left, wout[pl.ds(other * 1024, 1024), :], preferred_element_type=F32)
        total = total + res[pair].reshape(64, HD).astype(F32)
        hidden[pl.ds(pl.multiple_of(z * 64, 64), 64), :] = total

    def prepare():
        loads[3].wait()
        own.wait()
        for i in range(7):
            peer = lax.rem(a + 7 - i, 8)
            remote(res.at[peer], res.at[peer], rs.at[i], rr.at[i], (peer, f, t)).wait_recv()
            remote(cbuf.at[peer], cbuf.at[peer], es.at[i], er.at[i], (peer, f, t)).wait_recv()
        code = cbuf[0]
        for i in range(1, 8):
            code = code + cbuf[i]
        code = code - 1
        code_t = jnp.broadcast_to(code.astype(F32), (256, 256)).T.astype(jnp.int32)
        down, across = iota((256, 256), 0), iota((256, 256), 1)
        same = (code_t == code) & (down // 32 == across // 32)
        rank_row = jnp.sum(jnp.where(same & (down < across), 1.0, 0.0), axis=0, keepdims=True)
        rank_col = jnp.sum(jnp.where(same & (across < down), 1.0, 0.0), axis=1, keepdims=True)
        target_row = code * 8 + rank_row.astype(jnp.int32)
        target_col = code_t[:, 0:1] * 8 + rank_col.astype(jnp.int32)
        p, q_index = iota((512, 256), 0), iota((512, 256), 1)
        hit = ((p // 64) * 8 + lax.rem(p, 8) == target_row) & (lax.rem(p // 8, 8) == q_index // 32)
        place[...] = jnp.where(hit, 1.0, 0.0).astype(BF)
        q_index, p = iota((256, 512), 0), iota((256, 512), 1)
        hit = ((p // 64) * 8 + lax.rem(p, 8) == target_col) & (lax.rem(p // 8, 8) == q_index // 32)
        back_out[...] = jnp.where(hit, 1.0, 0.0).astype(BF)
        q_index, j = iota((256, 128), 0), iota((256, 128), 1)
        named = (code_t[:, :128] == j // 8) & (q_index // 32 == lax.rem(j, 8)) & (j < 64)
        tsend[...] = jnp.sum(jnp.where(named, 1.0, 0.0), axis=0, keepdims=True)
        tbuf[f] = tsend[...]

    first = [True]

    def prepared(z):
        if first[0]:
            prepare()
            for i, peer in enumerate(ffn_peers):
                copy = remote(tsend, tbuf.at[f], gs.at[i], gr.at[i], (a, peer, t))
                copy.start()
                sent.append(copy)
            first[0] = False
        consume(z)

    sent += gather_group(buf, 16, *gather_sems, prepared)
    routed = jnp.dot(place[...], hidden[...].astype(BF), preferred_element_type=F32).astype(BF)
    sbuf[...] = routed.reshape(8, 64, HD)
    for i, peer in enumerate(ffn_peers):
        copy = remote(sbuf.at[peer], hbuf.at[f], fs.at[i], fr.at[i], (a, peer, t))
        copy.start()
        sent.append(copy)
    hbuf[f] = sbuf[f]
    for i in range(7):
        peer = lax.rem(f + 7 - i, 8)
        remote(tbuf.at[peer], tbuf.at[peer], gs.at[i], gr.at[i], (a, peer, t)).wait_recv()
    table = tbuf[...].reshape(8, 128)
    table_out[...] = table
    sums = jnp.broadcast_to(jnp.sum(table, axis=0, keepdims=True), (16, 128)).astype(BF)
    fold = jnp.where(iota((128, 128), 0) // 8 == iota((128, 128), 1), 1.0, 0.0).astype(BF)
    totals = jnp.dot(sums, fold, preferred_element_type=F32)
    most = jnp.max(totals, axis=1, keepdims=True)[:8]
    need_out[...] = jnp.broadcast_to(most, (8, 128)).astype(jnp.int32)
    for i in range(7):
        peer = lax.rem(f + 7 - i, 8)
        remote(hbuf.at[peer], hbuf.at[peer], fs.at[i], fr.at[i], (a, peer, t)).wait_recv()
    h_out[...] = hbuf[...].reshape(512, HD)
    for copy in sent:
        copy.wait_send()


def ffn_kernel(
    rows,
    h_ref, hidden, back, table, gain, wg_hbm, wu_hbm, wd_hbm,
    stream_out, sums_out,
    wg, wu, wd, buf, gate, up, act, csend, crecv, part, y1s, y1r, y2s, y2r, zsend, zrecv, unplace, rsend, rbuf, final,
    line, in_sems, kcs, kcr, k1s, k1r, k2s, k2r, kzs, kzr, kbs, kbr, kas, kar, kys, kyr, *gather_sems,
):
    a, f, t = position()
    z, core = lax.div(a, 2), lax.rem(a, 2)
    right, left, opposite = lax.rem(t + 1, 4), lax.rem(t + 3, 4), lax.rem(t + 2, 4)
    sibling = a + 1 - 2 * core
    half = rows // 2
    blocks = rows // 128
    loads = []
    for i, (src, dst) in enumerate(((wg_hbm, wg), (wu_hbm, wu), (wd_hbm, wd))):
        copy = pltpu.make_async_copy(src, dst, in_sems.at[i])
        copy.start()
        loads.append(copy)
    attn_peers = [lax.rem(a + step, 8) for step in range(1, 8)]
    ffn_peers = [lax.rem(f + step, 8) for step in range(1, 8)]
    tp_peers = [lax.rem(t + step, 4) for step in range(1, 4)]

    all_here = greet(
        [(peer, f, t) for peer in attn_peers]
        + [(a, peer, t) for peer in ffn_peers]
        + [(a, f, peer) for peer in tp_peers]
    )

    j, p = iota((128, 512), 0), iota((128, 512), 1)
    pick = jnp.where(j == f * 8 + lax.rem(p // 8, 8), 1.0, 0.0).astype(BF)
    table16 = jnp.concatenate([table[...], table[...]], axis=0).astype(BF)
    counts = jnp.dot(table16, pick, preferred_element_type=F32)[:8]
    s, p = iota((8, 512), 0), iota((8, 512), 1)
    counts = jnp.sum(jnp.where(s == p // 64, counts, 0.0), axis=0, keepdims=True)
    live = lax.rem(iota((1, 512), 1), 8).astype(F32) < counts
    flags = jnp.broadcast_to(jnp.where(live, 1.0, 0.0), (16, 512)).astype(BF)
    before = jnp.where(iota((512, 512), 0) < iota((512, 512), 1), 1.0, 0.0).astype(BF)
    place = jnp.dot(flags, before, preferred_element_type=F32)[:1]
    place = jnp.where(live, place, -1.0).astype(jnp.int32)
    compact = jnp.where(iota((rows, 512), 0) == place, 1.0, 0.0).astype(BF)
    picked = jnp.dot(compact, h_ref[...], preferred_element_type=F32)
    slot = buf.at[a, t]
    slot[pl.ds(0, rows), :] = (picked * gain[...]).astype(BF)
    squares = picked * picked
    tail = jnp.zeros((16, 128), F32)
    line_index = iota((16, 128), 0)
    for i in range(blocks):
        block = jnp.sum(squares[i * 128 : (i + 1) * 128].T, axis=0, keepdims=True)
        high = block.astype(BF).astype(F32)
        tail = jnp.where(line_index == i, high, tail)
        tail = jnp.where(line_index == blocks + i, block - high, tail)
    slot[pl.ds(rows, 16), :] = tail.astype(BF)

    all_here()

    first = [True]

    def consume(chunk):
        if first[0]:
            loads[0].wait()
            loads[1].wait()
            place_t = jnp.broadcast_to(place.astype(F32), (128, 512)).T.astype(jnp.int32)
            for i in range(blocks):
                hit = place_t == iota((512, 128), 1) + i * 128
                unplace[:, pl.ds(i * 128, 128)] = jnp.where(hit, 1.0, 0.0).astype(BF)
        for c in range(2):
            index = chunk * 2 + c
            depth = pl.ds(pl.multiple_of(index * 512, 512), 512)
            for m in range(0, rows, 256):
                span = pl.ds(m, 256)
                lhs = jnp.concatenate([buf[index, other, span, :] for other in range(4)], axis=1)
                for weight, total in ((wg, gate), (wu, up)):
                    value = lax.dot_general(
                        lhs, weight[:, depth], (((1,), (1,)), ((), ())), preferred_element_type=F32
                    )
                    if first[0] and c == 0:
                        total[span, :] = value
                    else:
                        total[span, :] += value
        first[0] = False

    sent = gather_group(buf, half + 16, *gather_sems, consume)

    tails = jnp.sum(buf[:, :, pl.ds(rows, 16), :].astype(F32).reshape(32, 16, 128), axis=0)
    for i in range(blocks):
        span = pl.ds(i * 128, 128)
        total = tails[i : i + 1] + tails[blocks + i : blocks + i + 1]
        inverse = lax.rsqrt(total / 4096.0 + EPSILON)
        scale = jnp.broadcast_to(inverse, (128, 128)).T
        scale = jnp.concatenate([scale] * 4, axis=1)[:, :448]
        g = gate[span, :] * scale
        act[span, :] = (g / (1.0 + jnp.exp(-g)) * (up[span, :] * scale)).astype(BF)
    loads[2].wait()

    def start(copy):
        copy.start()
        sent.append(copy)

    def chunk_columns(dz, c):
        index = lax.rem(z + dz, 4) * 2 + c
        return pl.ds(pl.multiple_of(index * 512, 512), 512)

    def down(dz, c, store):
        for m in range(0, rows, 256):
            span = pl.ds(m, 256)
            store(span, jnp.dot(act[span, :], wd[:, chunk_columns(dz, c)], preferred_element_type=F32))

    def give(i):
        def store(span, value):
            csend[i, span, :] = value.astype(BF)

        down(RS_ORDER[i], 1 - core, store)
        start(remote(csend.at[i], crecv.at[i], kcs.at[i], kcr.at[i], (sibling, f, t)))

    def keep(i):
        def store(span, value):
            part[i, span, :] = value

        down(RS_ORDER[i], core, store)

    def lanes(index):
        return pl.ds(pl.multiple_of(index * HD, HD), HD)

    top, low = pl.ds(0, half), pl.ds(half, half)

    def y_first(i):
        remote(csend.at[i], crecv.at[i], kcs.at[i], kcr.at[i], (sibling, f, t)).wait_recv()
        part[i] += crecv[i].astype(F32)
        y1s[i, 0, top, :] = part[i, top, lanes(opposite)].astype(BF)
        y1s[i, 0, low, :] = part[i, low, lanes(right)].astype(BF)
        start(remote(y1s.at[i, 0], y1r.at[i, 0], k1s.at[i, 0], k1r.at[i, 0], (a, f, right)))
        y1s[i, 1, top, :] = part[i, top, lanes(left)].astype(BF)
        y1s[i, 1, low, :] = part[i, low, lanes(opposite)].astype(BF)
        start(remote(y1s.at[i, 1], y1r.at[i, 1], k1s.at[i, 1], k1r.at[i, 1], (a, f, left)))

    def y_second(i):
        remote(y1s.at[i, 0], y1r.at[i, 0], k1s.at[i, 0], k1r.at[i, 0], (a, f, right)).wait_recv()
        y2s[i, 0] = (part[i, top, lanes(right)] + y1r[i, 0, top, :].astype(F32)).astype(BF)
        start(remote(y2s.at[i, 0], y2r.at[i, 0], k2s.at[i, 0], k2r.at[i, 0], (a, f, right)))
        remote(y1s.at[i, 1], y1r.at[i, 1], k1s.at[i, 1], k1r.at[i, 1], (a, f, left)).wait_recv()
        y2s[i, 1] = (part[i, low, lanes(left)] + y1r[i, 1, low, :].astype(F32)).astype(BF)
        start(remote(y2s.at[i, 1], y2r.at[i, 1], k2s.at[i, 1], k2r.at[i, 1], (a, f, left)))

    def y_sum(i):
        remote(y2s.at[i, 0], y2r.at[i, 0], k2s.at[i, 0], k2r.at[i, 0], (a, f, right)).wait_recv()
        remote(y2s.at[i, 1], y2r.at[i, 1], k2s.at[i, 1], k2r.at[i, 1], (a, f, left)).wait_recv()
        upper = part[i, top, lanes(t)] + y1r[i, 1, top, :].astype(F32) + y2r[i, 0].astype(F32)
        lower = part[i, low, lanes(t)] + y1r[i, 0, low, :].astype(F32) + y2r[i, 1].astype(F32)
        return upper, lower

    def z_give(i):
        dz = RS_ORDER[i]
        upper, lower = y_sum(i)
        zsend[i, top, :] = upper.astype(BF)
        zsend[i, low, :] = lower.astype(BF)
        start(remote(zsend.at[i], zrecv.at[i], kzs.at[i], kzr.at[i], (lax.rem(a + 2 * dz, 8), f, t)))

    give(0)
    keep(0)
    give(1)
    keep(1)
    y_first(0)
    give(2)
    keep(2)
    y_first(1)
    give(3)
    y_second(0)
    keep(3)
    y_first(2)
    y_second(1)
    y_first(3)
    z_give(0)
    y_second(2)
    z_give(1)
    y_second(3)
    z_give(2)
    total = jnp.concatenate(y_sum(3), axis=0)
    for i in range(3):
        remote(zsend.at[i], zrecv.at[i], kzs.at[i], kzr.at[i], (sibling, f, t)).wait_recv()
        total = total + zrecv[i].astype(F32)

    sums_out[...] = jnp.sum(total, axis=0, keepdims=True)
    spread = jnp.dot(unplace[...], total.astype(BF), preferred_element_type=F32).astype(BF)
    rsend[...] = spread.reshape(8, 64, HD)
    for i, peer in enumerate(ffn_peers):
        start(remote(rsend.at[peer], rbuf.at[f], kbs.at[i], kbr.at[i], (a, peer, t)))
    rbuf[f] = rsend[f]
    live_rows = jnp.sum(back[...].astype(F32), axis=1, keepdims=True) > 0.5
    for i in range(7):
        peer = lax.rem(f + 7 - i, 8)
        remote(rbuf.at[peer], rbuf.at[peer], kbs.at[i], kbr.at[i], (a, peer, t)).wait_recv()
    returned = jnp.dot(back[...], rbuf[...].reshape(512, HD), preferred_element_type=F32)
    line[...] = jnp.where(live_rows, hidden[...] + returned, 0.0).astype(BF).reshape(8, 32, HD)
    for i, peer in enumerate(attn_peers):
        start(remote(line.at[peer], final.at[t, a], kas.at[i], kar.at[i], (peer, f, t)))
    final[t, a] = line[a]
    for i in range(7):
        peer = lax.rem(a + 7 - i, 8)
        remote(final.at[t, peer], final.at[t, peer], kas.at[i], kar.at[i], (peer, f, t)).wait_recv()
    for i, peer in enumerate(tp_peers):
        start(remote(final.at[t], final.at[t], kys.at[i], kyr.at[i], (a, f, peer)))
    for i in range(3):
        peer = lax.rem(t + 3 - i, 4)
        remote(final.at[peer], final.at[peer], kys.at[i], kyr.at[i], (a, f, peer)).wait_recv()
    for other in range(4):
        for source in range(8):
            stream_out[:, pl.ds((source * 4 + other) * HD, HD)] = final[other, source]
    for copy in sent:
        copy.wait_send()


VMEM = pl.BlockSpec(memory_space=pltpu.VMEM)
ANY = pl.BlockSpec(memory_space=pl.ANY)
DMA = pltpu.SemaphoreType.DMA


def project(*operands):
    return pl.pallas_call(
        project_kernel,
        name="project",
        out_shape=(
            jax.ShapeDtypeStruct((512, HD), BF),
            jax.ShapeDtypeStruct((256, HD), F32),
            jax.ShapeDtypeStruct((256, 512), BF),
            jax.ShapeDtypeStruct((8, 128), F32),
            jax.ShapeDtypeStruct((8, 128), jnp.int32),
        ),
        in_specs=[ANY, ANY, ANY, VMEM, VMEM, ANY, ANY],
        out_specs=[VMEM] * 5,
        scratch_shapes=[
            pltpu.VMEM((32, 1024), BF),
            pltpu.VMEM((32, 128, HD), BF),
            pltpu.VMEM((32, 128, HD), BF),
            pltpu.VMEM((4096, HD), BF),
            pltpu.VMEM((8, 4, 32, 1024), BF),
            pltpu.VMEM((8, 32, HD), BF),
            pltpu.VMEM((8, 1, 256), jnp.int32),
            pltpu.VMEM((512, 256), BF),
            pltpu.VMEM((8, 64, HD), BF),
            pltpu.VMEM((8, 64, HD), BF),
            pltpu.VMEM((1, 128), F32),
            pltpu.VMEM((8, 1, 128), F32),
            DMA((4,)),
            *[DMA((7,)) for _ in range(8)],
            DMA(()),
            *GATHER_SEMS,
        ],
        compiler_params=pltpu.CompilerParams(
            collective_id=0, has_side_effects=True, vmem_limit_bytes=60 * 2**20
        ),
    )(*operands)


def feed_forward(rows, identity, *operands):
    return pl.pallas_call(
        functools.partial(ffn_kernel, rows),
        name=f"feed_forward_{rows}",
        out_shape=(
            jax.ShapeDtypeStruct((32, 4096), BF),
            jax.ShapeDtypeStruct((1, HD), F32),
        ),
        in_specs=[VMEM] * 5 + [ANY] * 3,
        out_specs=[VMEM] * 2,
        scratch_shapes=[
            pltpu.VMEM((448, 4096), BF),
            pltpu.VMEM((448, 4096), BF),
            pltpu.VMEM((448, 4096), BF),
            pltpu.VMEM((8, 4, rows + 16, HD), BF),
            pltpu.VMEM((rows, 448), F32),
            pltpu.VMEM((rows, 448), F32),
            pltpu.VMEM((rows, 448), BF),
            pltpu.VMEM((4, rows, 512), BF),
            pltpu.VMEM((4, rows, 512), BF),
            pltpu.VMEM((4, rows, 512), F32),
            pltpu.VMEM((4, 2, rows, HD), BF),
            pltpu.VMEM((4, 2, rows, HD), BF),
            pltpu.VMEM((4, 2, rows // 2, HD), BF),
            pltpu.VMEM((4, 2, rows // 2, HD), BF),
            pltpu.VMEM((3, rows, HD), BF),
            pltpu.VMEM((3, rows, HD), BF),
            pltpu.VMEM((512, rows), BF),
            pltpu.VMEM((8, 64, HD), BF),
            pltpu.VMEM((8, 64, HD), BF),
            pltpu.VMEM((4, 8, 32, HD), BF),
            pltpu.VMEM((8, 32, HD), BF),
            DMA((3,)),
            DMA((4,)),
            DMA((4,)),
            *[DMA((4, 2)) for _ in range(4)],
            DMA((3,)),
            DMA((3,)),
            *[DMA((7,)) for _ in range(4)],
            DMA((3,)),
            DMA((3,)),
            *GATHER_SEMS,
        ],
        compiler_params=pltpu.CompilerParams(
            collective_id=identity, has_side_effects=True, vmem_limit_bytes=56 * 2**20
        ),
    )(*operands)


def per_device(
    queries, keys, values, lengths, routes, residual, w_out, norm_gain, w_gate, w_up, w_down
):
    a = lax.axis_index("attn")
    lens = jnp.broadcast_to(lengths[:, None], (32, 128))
    code = jnp.where(lengths > 0, routes[:, 0], 8) + 1
    codes = jnp.where(iota((8, 32), 0) == a, code[None, :], 0).reshape(1, 256)
    h, hidden, back, table, need = project(queries, keys, values, lens, codes, residual, w_out)
    operands = (h, hidden, back, table, norm_gain[None, :], w_gate[0].T, w_up[0].T, w_down[0])
    return lax.cond(
        need[0, 0] <= 256,
        functools.partial(feed_forward, 256, 1),
        functools.partial(feed_forward, 512, 2),
        *operands,
    )


def solution(mesh):
    placed = (
        P(("attn", "ffn"), "tp"),
        P(("attn", "ffn"), None, "tp"),
        P(("attn", "ffn"), None, "tp"),
        P(("attn", "ffn")),
        P(("attn", "ffn"), None),
        P(("attn", "ffn"), None),
        P(None, ("attn", "tp")),
        P(("attn", "tp")),
        P("ffn", None, ("attn", "tp")),
        P("ffn", None, ("attn", "tp")),
        P("ffn", ("attn", "tp"), None),
    )
    return jax.shard_map(
        per_device,
        mesh=mesh,
        in_specs=placed,
        out_specs=(P(("attn", "ffn"), None), P("ffn", ("attn", "tp"))),
        check_vma=False,
    )
```

time: 412 us -> 105 us (0.25)
  waiting for transfers between devices: 186 us -> 0 us
  blocking collectives: 164 us -> 0 us
  Pallas kernels: 0 us -> 97.6 us
  matrix products: 24.6 us -> 0 us
  between operations: 13.9 us -> 1.31 us
  other arithmetic: 9.78 us -> 0.76 us
  local copies, waits for them, and re-layouts: 9.72 us -> 4.39 us
    pallas_call x0 -> x2, Pallas kernels: none -> 97.6 us  [the longest x1 58.5 us: feed_forward(): pl.pallas_call(functools.partial(ffn_kernel, rows), name=f'feed_forward_{...]
    unnamed x4 -> x0, waiting for transfers between devices: 95.1 us -> none
    all_gather x2 -> x0, waiting for transfers between devices: 91.1 us -> none  [the longest x1 67.9 us: per_device(): shard_cols = lax.all_gather(normed, ('attn', 'tp'), axis=1, tiled=True)]
    all_to_all x5 -> x0, blocking collectives: 70.4 us -> none  [the longest x1 25.2 us: per_device(): lax.all_to_all(recv_x, 'attn', split_axis=1, concat_axis=0, tiled=True)]
    psum x1 -> x0, blocking collectives: 70.1 us -> none  [per_device(): squares = lax.psum(jnp.sum(hidden * hidden, axis=1), ('attn', 'tp'))]
    dot_general x8 -> x0, matrix products: 24.6 us -> none  [the longest x1 10.7 us: per_device(): jnp.dot(activated, down_weights, preferred_element_type=jnp.float32)]
    all_gather x2 -> x0, blocking collectives: 23.2 us -> none  [the longest x1 11.6 us: per_device(): lax.all_gather(swapped.reshape(buffer_rows, attn_size, 1, block_width), '...]
    unnamed x10 -> x2, local copies, waits for them, and re-layouts: 8.45 us -> 1.22 us
  transfers between devices with their start and end apart: 3 -> 0, of which waited for: 3 -> 0; matrix products, arithmetic and copies ran while one was open for 0% -> 0% of each run, Pallas kernels for 0% -> 0%
where the time goes in v1:
time: 105 us; the launch traced here: 104 us
  Pallas kernels  97.6 us (93%)
  local copies, waits for them, and re-layouts  4.39 us (4%)
  between operations  1.31 us (1%)
    pallas_call x1, Pallas kernels, feed_forward(): pl.pallas_call(functools.partial(ffn_kernel, rows), name=f'feed_forward_{...  58.5 us
    pallas_call x1, Pallas kernels, project(): pl.pallas_call(project_kernel, name='project', out_shape=(jax.ShapeDtypeS...  39.1 us

profile of v1, /device:TPU:1, one launch (start us, length us, event | category | flops | bytes accessed | tf_op | source)
XLA Modules:
  0.0 104.5 jit_solution(9607011305722261885)
XLA Ops:
  0.6 0.7 fusion
  1.3 0.1 broadcast_select_fusion
  1.4 0.7 select_n.20.codes
  2.1 1.3 %broadcast_in_dim.26.lens = s32[32,128]{1,0:T(8,128)} broadcast(s32[32]{0:T(128)} %param.16), dimensions={0} | broadcast | bytes 16512 | tf_op jit(solution)/shard_map/broadcast_in_dim | solution.py:577
  3.4 39.1 %project.1 = (bf16[512,128]{1,0:T(8,128)(2,1)S(1)}, f32[256,128]{1,0:T(8,128)S(1)}, bf16[256,512]{1,0:T(8,128)(2,1)S(1)}, f32[8,128]{1,0:T(8,128)S(1)}, s32[8,128]{1,0:T(8,128)}) custom-call(bf16[32,1024]{1,0:T(8,128)(2,1)} %q_hbm.1, bf16[32,128,128]{2,1,0:T(8,128)(2,1)} %k_hbm.1, bf16[32,128,128]{2,1,0:T(8,128)(2,1)} %v_hbm.1, ...), custom_call_target="tpu_custom_call" | custom-call | tf_op jit(solution)/shard_map/project/pallas_call | solution.py:488
  42.5 1.2 %slice.3 = s32[1,1]{1,0:T(1,128)} slice(s32[8,128]{1,0:T(8,128)} %get-tuple-element.55), slice={[0:1], [0:1]} | slice | bytes 8 | tf_op jit(solution)/shard_map/slice | solution.py:583
  44.3 58.9 %conditional.1 = ((bf16[32,4096]{1,0:T(8,128)(2,1)S(1)}, f32[1,128]{1,0:T(1,128)S(1)})) conditional(s32[]{:T(128)} %bitcast.5, (bf16[512,128]{1,0:T(8,128)(2,1)S(1)}, f32[256,128]{1,0:T(8,128)S(1)}, bf16[256,512]{1,0:T(8,128)(2,1)S(1)}, f32[8,128]{1,0:T(8,128)S(1)}, f32[128]{0:T(128)}, /*index=5*/bf16[448,4096]{1,0:T(8,128)(2,1)}, ...), branch_computations={%region_0.1_spmd, %region_1.2_spmd} | conditional | bytes 8 | solution.py:582
  44.7 58.5 %feed_forward_256.1 = (bf16[32,4096]{1,0:T(8,128)(2,1)S(1)}, f32[1,128]{1,0:T(1,128)S(1)}) custom-call(bf16[512,128]{1,0:T(8,128)(2,1)S(1)} %get-tuple-element.40.h_ref, f32[256,128]{1,0:T(8,128)S(1)} %get-tuple-element.41.hidden, bf16[256,512]{1,0:T(8,128)(2,1)S(1)} %get-tuple-element.42.back, f32[8,128]{1,0:T(8,128)S(1)} %get-tuple-element.43.table, ...), custom_call_target="tpu_custom_call" | custom-call | tf_op jit(solution)/shard_map/cond/branch_1_fun/feed_forward_256/pallas_call | solution.py:525
  103.2 0.7 copy.27
  103.9 0.5 copy.28
  (1 shorter events, 0.0 us)

commit v2 on v1

--- a/solution.py
+++ b/solution.py
@@ -38,7 +38,7 @@
     return lambda: pl.semaphore_wait(barrier, len(devices))
 
 
-def gather_group(buf, half, zs, zr, ys, yr, hs, hr, cs, cr, consume):
+def gather_group(buf, half, zs, zr, ys, yr, hs, hr, cs, cr, consume, meanwhile=None):
     a, f, t = position()
     right, left = lax.rem(t + 1, 4), lax.rem(t + 3, 4)
     opposite = lax.rem(t + 2, 4)
@@ -63,10 +63,16 @@
         slot = buf.at[source[k], t]
         start(remote(slot, slot, ys.at[k, 0], yr.at[k, 0], (a, f, right)))
         start(remote(slot, slot, ys.at[k, 1], yr.at[k, 1], (a, f, left)))
+        if k == 3:
+            start(remote(slot, slot, hs.at[k, 0], hr.at[k, 0], (a, f, opposite)))
 
     def y_forward(k):
         slot = buf.at[source[k], left]
         remote(slot, slot, ys.at[k, 0], yr.at[k, 0], (a, f, right)).wait_recv()
+        if k == 3:
+            slot = buf.at[source[k], right]
+            remote(slot, slot, ys.at[k, 1], yr.at[k, 1], (a, f, left)).wait_recv()
+            return
         piece = slot.at[first]
         start(remote(piece, piece, hs.at[k, 0], hr.at[k, 0], (a, f, right)))
         slot = buf.at[source[k], right]
@@ -76,6 +82,11 @@
 
     def core_send(k):
         slot = buf.at[source[k], opposite]
+        if k == 3:
+            remote(slot, slot, hs.at[k, 0], hr.at[k, 0], (a, f, opposite)).wait_recv()
+            chunk = buf.at[source[k]]
+            start(remote(chunk, chunk, cs.at[k], cr.at[k], (sibling, f, t)))
+            return
         remote(slot.at[first], slot.at[first], hs.at[k, 0], hr.at[k, 0], (a, f, right)).wait_recv()
         remote(slot.at[second], slot.at[second], hs.at[k, 1], hr.at[k, 1], (a, f, left)).wait_recv()
         chunk = buf.at[source[k]]
@@ -90,6 +101,8 @@
     for k in range(3):
         z_send(k)
     y_send(0)
+    if meanwhile is not None:
+        sent.extend(meanwhile())
     z_wait(0)
     y_send(1)
     y_forward(0)
@@ -154,45 +167,107 @@
 
 
 def project_kernel(
-    q_hbm, k_hbm, v_hbm, lens, codes, res_hbm, wout_hbm,
-    h_out, hidden, back_out, table_out, need_out,
-    q, k, v, wout, buf, res, cbuf, place, sbuf, hbuf, tsend, tbuf,
+    q_hbm, k_hbm, v_hbm, len_hbm, route_hbm, res_hbm, wout_hbm,
+    h_out, hidden, back_out, table_out, small_out,
+    q, k, v, wout, lens, routes, wide, codes, buf, res, cbuf, place, sbuf, hbuf, tsend, tbuf,
     in_sems, rs, rr, es, er, fs, fr, gs, gr, own_sem, *gather_sems,
 ):
     a, f, t = position()
-    loads = []
-    for i, (src, dst) in enumerate(((q_hbm, q), (k_hbm, k), (v_hbm, v), (wout_hbm, wout))):
-        copy = pltpu.make_async_copy(src, dst, in_sems.at[i])
-        copy.start()
-        loads.append(copy)
     attn_peers = [lax.rem(a + step, 8) for step in range(1, 8)]
     ffn_peers = [lax.rem(f + step, 8) for step in range(1, 8)]
     all_here = greet(
         [(peer, f, t) for peer in attn_peers]
         + [(a, peer, t) for peer in ffn_peers]
-        + [(a, f, lax.rem(t + 1, 4)), (a, f, lax.rem(t + 3, 4))]
-    )
-    all_here()
+        + [(a, f, lax.rem(t + step, 4)) for step in range(1, 4)]
+    )
+    loads = []
+    pairs = (
+        (len_hbm, lens), (route_hbm, routes), (q_hbm, q), (k_hbm, k), (v_hbm, v), (wout_hbm, wout),
+    )
+    for i, (src, dst) in enumerate(pairs):
+        copy = pltpu.make_async_copy(src, dst, in_sems.at[i])
+        copy.start()
+        loads.append(copy)
 
     def columns(index):
         return pl.ds(pl.multiple_of((index * 4 + t) * HD, HD), HD)
 
-    sent = []
+    loads[0].wait()
+    loads[1].wait()
+    wide[...] = jnp.zeros((8, 128), F32)
+    wide[0:1, 0:32] = lens[...].astype(F32)
+    wide[1:2, 0:32] = jnp.where(lens[...] > 0, routes[...], 8).astype(F32) + 1.0
+    limits = jnp.broadcast_to(wide[0:1, :], (128, 128)).T[:32].astype(jnp.int32)
+    tile = jnp.where(iota((128, 256), 0) == lax.rem(iota((128, 256), 1), 32), 1.0, 0.0).astype(BF)
+    tiled = jnp.dot(jnp.broadcast_to(wide[1:2, :], (16, 128)).astype(BF), tile, preferred_element_type=F32)
+    codes[...] = jnp.where(iota((1, 256), 1) // 32 == a, tiled[:1], 0.0)
+    for copy in loads[2:5]:
+        copy.wait()
+    attend(q, k, v, limits, buf.at[a, t])
     cbuf[a] = codes[...]
-    for i, peer in enumerate(attn_peers):
-        copy = remote(res_hbm.at[:, columns(peer)], res.at[a], rs.at[i], rr.at[i], (peer, f, t))
-        copy.start()
-        sent.append(copy)
-        copy = remote(codes, cbuf.at[a], es.at[i], er.at[i], (peer, f, t))
-        copy.start()
-        sent.append(copy)
     own = pltpu.make_async_copy(res_hbm.at[:, columns(a)], res.at[a], own_sem)
     own.start()
-    for copy in loads[:3]:
-        copy.wait()
-    attend(q, k, v, lens, buf.at[a, t])
+    all_here()
+
+    def exchange():
+        sent = []
+        for i, peer in enumerate(attn_peers):
+            copy = remote(codes, cbuf.at[a], es.at[i], er.at[i], (peer, f, t))
+            copy.start()
+            sent.append(copy)
+            copy = remote(res_hbm.at[:, columns(peer)], res.at[a], rs.at[i], rr.at[i], (peer, f, t))
+            copy.start()
+            sent.append(copy)
+        return sent
+
+    def prepare():
+        loads[5].wait()
+        own.wait()
+        for i in range(7):
+            peer = lax.rem(a + 7 - i, 8)
+            remote(cbuf.at[peer], cbuf.at[peer], es.at[i], er.at[i], (peer, f, t)).wait_recv()
+        code = cbuf[0]
+        for i in range(1, 8):
+            code = code + cbuf[i]
+        code = code - 1.0
+        code_t = jnp.broadcast_to(code, (256, 256)).T
+        down, across = iota((256, 256), 0), iota((256, 256), 1)
+        same = (code_t == code) & (down // 32 == across // 32)
+        rank_row = jnp.sum(jnp.where(same & (down < across), 1.0, 0.0), axis=0, keepdims=True)
+        rank_col = jnp.sum(jnp.where(same & (across < down), 1.0, 0.0), axis=1, keepdims=True)
+        target_row = (code * 8.0 + rank_row).astype(jnp.int32)
+        target_col = (code_t[:, 0:1] * 8.0 + rank_col).astype(jnp.int32)
+        p, q_index = iota((512, 64), 0), iota((512, 64), 1)
+        wanted = (lax.rem(p, 128) // 16) * 8 + lax.rem(p, 8)
+        of_z = jnp.concatenate(
+            [jnp.broadcast_to(target_row[:, z * 64 : (z + 1) * 64], (128, 64)) for z in range(4)], axis=0
+        )
+        hit = (wanted == of_z) & (lax.rem(p // 8, 2) == q_index // 32)
+        place[...] = jnp.where(hit, 1.0, 0.0).astype(BF).reshape(4, 128, 64)
+        q_index, p = iota((256, 512), 0), iota((256, 512), 1)
+        hit = ((p // 64) * 8 + lax.rem(p, 8) == target_col) & (lax.rem(p // 8, 8) == q_index // 32)
+        back_out[...] = jnp.where(hit, 1.0, 0.0).astype(BF)
+        q_index, j = iota((256, 128), 0), iota((256, 128), 1)
+        block = (q_index // 32 == lax.rem(j, 8)) & (j < 64)
+        named = (code_t[:, :128] == (j // 8).astype(F32)) & block
+        tsend[...] = jnp.sum(jnp.where(named, 1.0, 0.0), axis=0, keepdims=True)
+        tbuf[f] = tsend[...]
+        for i in range(7):
+            peer = lax.rem(a + 7 - i, 8)
+            remote(res.at[peer], res.at[peer], rs.at[i], rr.at[i], (peer, f, t)).wait_recv()
+
+    later = []
+    chunks = []
 
     def consume(z):
+        if not chunks:
+            prepare()
+            for i, peer in enumerate(ffn_peers):
+                copy = remote(tsend, tbuf.at[f], gs.at[i], gr.at[i], (a, peer, t))
+                copy.start()
+                later.append(copy)
+        number = len(chunks)
+        chunks.append(z)
         pair = pl.ds(2 * z, 2)
         total = jnp.zeros((64, HD), F32)
         for other in range(4):
@@ -200,56 +275,16 @@
             total = total + jnp.dot(left, wout[pl.ds(other * 1024, 1024), :], preferred_element_type=F32)
         total = total + res[pair].reshape(64, HD).astype(F32)
         hidden[pl.ds(pl.multiple_of(z * 64, 64), 64), :] = total
-
-    def prepare():
-        loads[3].wait()
-        own.wait()
-        for i in range(7):
-            peer = lax.rem(a + 7 - i, 8)
-            remote(res.at[peer], res.at[peer], rs.at[i], rr.at[i], (peer, f, t)).wait_recv()
-            remote(cbuf.at[peer], cbuf.at[peer], es.at[i], er.at[i], (peer, f, t)).wait_recv()
-        code = cbuf[0]
-        for i in range(1, 8):
-            code = code + cbuf[i]
-        code = code - 1
-        code_t = jnp.broadcast_to(code.astype(F32), (256, 256)).T.astype(jnp.int32)
-        down, across = iota((256, 256), 0), iota((256, 256), 1)
-        same = (code_t == code) & (down // 32 == across // 32)
-        rank_row = jnp.sum(jnp.where(same & (down < across), 1.0, 0.0), axis=0, keepdims=True)
-        rank_col = jnp.sum(jnp.where(same & (across < down), 1.0, 0.0), axis=1, keepdims=True)
-        target_row = code * 8 + rank_row.astype(jnp.int32)
-        target_col = code_t[:, 0:1] * 8 + rank_col.astype(jnp.int32)
-        p, q_index = iota((512, 256), 0), iota((512, 256), 1)
-        hit = ((p // 64) * 8 + lax.rem(p, 8) == target_row) & (lax.rem(p // 8, 8) == q_index // 32)
-        place[...] = jnp.where(hit, 1.0, 0.0).astype(BF)
-        q_index, p = iota((256, 512), 0), iota((256, 512), 1)
-        hit = ((p // 64) * 8 + lax.rem(p, 8) == target_col) & (lax.rem(p // 8, 8) == q_index // 32)
-        back_out[...] = jnp.where(hit, 1.0, 0.0).astype(BF)
-        q_index, j = iota((256, 128), 0), iota((256, 128), 1)
-        named = (code_t[:, :128] == j // 8) & (q_index // 32 == lax.rem(j, 8)) & (j < 64)
-        tsend[...] = jnp.sum(jnp.where(named, 1.0, 0.0), axis=0, keepdims=True)
-        tbuf[f] = tsend[...]
-
-    first = [True]
-
-    def prepared(z):
-        if first[0]:
-            prepare()
-            for i, peer in enumerate(ffn_peers):
-                copy = remote(tsend, tbuf.at[f], gs.at[i], gr.at[i], (a, peer, t))
-                copy.start()
-                sent.append(copy)
-            first[0] = False
-        consume(z)
-
-    sent += gather_group(buf, 16, *gather_sems, prepared)
-    routed = jnp.dot(place[...], hidden[...].astype(BF), preferred_element_type=F32).astype(BF)
-    sbuf[...] = routed.reshape(8, 64, HD)
-    for i, peer in enumerate(ffn_peers):
-        copy = remote(sbuf.at[peer], hbuf.at[f], fs.at[i], fr.at[i], (a, peer, t))
-        copy.start()
-        sent.append(copy)
-    hbuf[f] = sbuf[f]
+        routed = jnp.dot(place[z], total.astype(BF), preferred_element_type=F32).astype(BF)
+        sbuf[z] = routed.reshape(8, 16, HD)
+        for i, peer in enumerate(ffn_peers):
+            copy = remote(sbuf.at[z, peer], hbuf.at[f, z], fs.at[number, i], fr.at[number, i], (a, peer, t))
+            copy.start()
+            later.append(copy)
+        hbuf[f, z] = sbuf[z, f]
+
+    sent = gather_group(buf, 16, *gather_sems, consume, exchange)
+    sent += later
     for i in range(7):
         peer = lax.rem(f + 7 - i, 8)
         remote(tbuf.at[peer], tbuf.at[peer], gs.at[i], gr.at[i], (a, peer, t)).wait_recv()
@@ -258,11 +293,12 @@
     sums = jnp.broadcast_to(jnp.sum(table, axis=0, keepdims=True), (16, 128)).astype(BF)
     fold = jnp.where(iota((128, 128), 0) // 8 == iota((128, 128), 1), 1.0, 0.0).astype(BF)
     totals = jnp.dot(sums, fold, preferred_element_type=F32)
-    most = jnp.max(totals, axis=1, keepdims=True)[:8]
-    need_out[...] = jnp.broadcast_to(most, (8, 128)).astype(jnp.int32)
-    for i in range(7):
-        peer = lax.rem(f + 7 - i, 8)
-        remote(hbuf.at[peer], hbuf.at[peer], fs.at[i], fr.at[i], (a, peer, t)).wait_recv()
+    small_out[0, 0] = jnp.where(jnp.max(totals) <= 256.0, 1, 0)
+    for number, z in enumerate(chunks):
+        for i in range(7):
+            peer = lax.rem(f + 7 - i, 8)
+            slot = hbuf.at[peer, z]
+            remote(slot, slot, fs.at[number, i], fr.at[number, i], (a, peer, t)).wait_recv()
     h_out[...] = hbuf[...].reshape(512, HD)
     for copy in sent:
         copy.wait_send()
@@ -461,17 +497,30 @@
         remote(rbuf.at[peer], rbuf.at[peer], kbs.at[i], kbr.at[i], (a, peer, t)).wait_recv()
     returned = jnp.dot(back[...], rbuf[...].reshape(512, HD), preferred_element_type=F32)
     line[...] = jnp.where(live_rows, hidden[...] + returned, 0.0).astype(BF).reshape(8, 32, HD)
-    for i, peer in enumerate(attn_peers):
-        start(remote(line.at[peer], final.at[t, a], kas.at[i], kar.at[i], (peer, f, t)))
+    for step in (0, 1, 3, 2):
+        for cross in (1, 0):
+            if step or cross:
+                peer = lax.rem(z + step, 4) * 2 + (1 - core if cross else core)
+                copy = remote(
+                    line.at[peer], final.at[t, a], kas.at[step, cross], kar.at[step, cross], (peer, f, t)
+                )
+                start(copy)
     final[t, a] = line[a]
-    for i in range(7):
-        peer = lax.rem(a + 7 - i, 8)
-        remote(final.at[t, peer], final.at[t, peer], kas.at[i], kar.at[i], (peer, f, t)).wait_recv()
-    for i, peer in enumerate(tp_peers):
-        start(remote(final.at[t], final.at[t], kys.at[i], kyr.at[i], (a, f, peer)))
-    for i in range(3):
-        peer = lax.rem(t + 3 - i, 4)
-        remote(final.at[peer], final.at[peer], kys.at[i], kyr.at[i], (a, f, peer)).wait_recv()
+    for step in (0, 1, 3, 2):
+        from_z = lax.rem(z + 4 - step, 4)
+        for cross in (1, 0):
+            if step or cross:
+                slot = final.at[t, from_z * 2 + (1 - core if cross else core)]
+                remote(slot, slot, kas.at[step, cross], kar.at[step, cross], (sibling, f, t)).wait_recv()
+        slot = final.at[t, pl.ds(2 * from_z, 2)]
+        for i, peer in enumerate(tp_peers):
+            start(remote(slot, slot, kys.at[step, i], kyr.at[step, i], (a, f, peer)))
+    for step in (0, 1, 3, 2):
+        from_z = lax.rem(z + 4 - step, 4)
+        for i in range(3):
+            peer = lax.rem(t + 3 - i, 4)
+            slot = final.at[peer, pl.ds(2 * from_z, 2)]
+            remote(slot, slot, kys.at[step, i], kyr.at[step, i], (a, f, peer)).wait_recv()
     for other in range(4):
         for source in range(8):
             stream_out[:, pl.ds((source * 4 + other) * HD, HD)] = final[other, source]
@@ -493,25 +542,33 @@
             jax.ShapeDtypeStruct((256, HD), F32),
             jax.ShapeDtypeStruct((256, 512), BF),
             jax.ShapeDtypeStruct((8, 128), F32),
-            jax.ShapeDtypeStruct((8, 128), jnp.int32),
+            jax.ShapeDtypeStruct((1, 1), jnp.int32),
         ),
-        in_specs=[ANY, ANY, ANY, VMEM, VMEM, ANY, ANY],
-        out_specs=[VMEM] * 5,
+        in_specs=[ANY] * 7,
+        out_specs=[VMEM] * 4 + [pl.BlockSpec(memory_space=pltpu.SMEM)],
         scratch_shapes=[
             pltpu.VMEM((32, 1024), BF),
             pltpu.VMEM((32, 128, HD), BF),
             pltpu.VMEM((32, 128, HD), BF),
             pltpu.VMEM((4096, HD), BF),
+            pltpu.VMEM((1, 32), jnp.int32),
+            pltpu.VMEM((1, 32), jnp.int32),
+            pltpu.VMEM((8, 128), F32),
+            pltpu.VMEM((1, 256), F32),
             pltpu.VMEM((8, 4, 32, 1024), BF),
             pltpu.VMEM((8, 32, HD), BF),
-            pltpu.VMEM((8, 1, 256), jnp.int32),
-            pltpu.VMEM((512, 256), BF),
-            pltpu.VMEM((8, 64, HD), BF),
-            pltpu.VMEM((8, 64, HD), BF),
+            pltpu.VMEM((8, 1, 256), F32),
+            pltpu.VMEM((4, 128, 64), BF),
+            pltpu.VMEM((4, 8, 16, HD), BF),
+            pltpu.VMEM((8, 4, 16, HD), BF),
             pltpu.VMEM((1, 128), F32),
             pltpu.VMEM((8, 1, 128), F32),
-            DMA((4,)),
-            *[DMA((7,)) for _ in range(8)],
+            DMA((6,)),
+            *[DMA((7,)) for _ in range(4)],
+            DMA((4, 7)),
+            DMA((4, 7)),
+            DMA((7,)),
+            DMA((7,)),
             DMA(()),
             *GATHER_SEMS,
         ],
@@ -559,9 +616,12 @@
             *[DMA((4, 2)) for _ in range(4)],
             DMA((3,)),
             DMA((3,)),
-            *[DMA((7,)) for _ in range(4)],
-            DMA((3,)),
-            DMA((3,)),
+            DMA((7,)),
+            DMA((7,)),
+            DMA((4, 2)),
+            DMA((4, 2)),
+            DMA((4, 3)),
+            DMA((4, 3)),
             *GATHER_SEMS,
         ],
         compiler_params=pltpu.CompilerParams(
@@ -573,14 +633,12 @@
 def per_device(
     queries, keys, values, lengths, routes, residual, w_out, norm_gain, w_gate, w_up, w_down
 ):
-    a = lax.axis_index("attn")
-    lens = jnp.broadcast_to(lengths[:, None], (32, 128))
-    code = jnp.where(lengths > 0, routes[:, 0], 8) + 1
-    codes = jnp.where(iota((8, 32), 0) == a, code[None, :], 0).reshape(1, 256)
-    h, hidden, back, table, need = project(queries, keys, values, lens, codes, residual, w_out)
+    h, hidden, back, table, small = project(
+        queries, keys, values, lengths.reshape(1, 32), routes.reshape(1, 32), residual, w_out
+    )
     operands = (h, hidden, back, table, norm_gain[None, :], w_gate[0].T, w_up[0].T, w_down[0])
     return lax.cond(
-        need[0, 0] <= 256,
+        small[0, 0] == 1,
         functools.partial(feed_forward, 256, 1),
         functools.partial(feed_forward, 512, 2),
         *operands,

time: 105 us -> 94.3 us (0.90)
  Pallas kernels: 97.6 us -> 91.3 us
  local copies, waits for them, and re-layouts: 4.39 us -> 1.22 us
    pallas_call x1, Pallas kernels: 39.1 us -> 34.9 us  [project(): pl.pallas_call(project_kernel, name='project', out_shape=(jax.ShapeDtypeS...]
    pallas_call x1, Pallas kernels: 58.5 us -> 56.4 us  [feed_forward(): pl.pallas_call(functools.partial(ffn_kernel, rows), name=f'feed_forward_{...]
    broadcast_in_dim x1 -> x0, local copies, waits for them, and re-layouts: 1.33 us -> none  [per_device(): lens = jnp.broadcast_to(lengths[:, None], (32, 128))]
    slice x1 -> x0, local copies, waits for them, and re-layouts: 1.19 us -> none  [per_device(): need[0, 0] <= 256]
where the time goes in v2:
time: 94.3 us; the launch traced here: 94.2 us
  Pallas kernels  91.3 us (97%)
  between operations  1.27 us (1%)
  local copies, waits for them, and re-layouts  1.22 us (1%)
    pallas_call x1, Pallas kernels, feed_forward(): pl.pallas_call(functools.partial(ffn_kernel, rows), name=f'feed_forward_{...  56.4 us
    pallas_call x1, Pallas kernels, project(): pl.pallas_call(project_kernel, name='project', out_shape=(jax.ShapeDtypeS...  34.9 us

profile of v2, /device:TPU:1, one launch (start us, length us, event | category | flops | bytes accessed | tf_op | source)
XLA Modules:
  0.0 94.2 jit_solution(8494665281608227953)
XLA Ops:
  0.6 34.9 %project.1 = (bf16[512,128]{1,0:T(8,128)(2,1)S(1)}, f32[256,128]{1,0:T(8,128)S(1)}, bf16[256,512]{1,0:T(8,128)(2,1)S(1)}, f32[8,128]{1,0:T(8,128)S(1)}, s32[1,1]{1,0:T(1,128)}) custom-call(bf16[32,1024]{1,0:T(8,128)(2,1)} %q_hbm.1, bf16[32,128,128]{2,1,0:T(8,128)(2,1)} %k_hbm.1, bf16[32,128,128]{2,1,0:T(8,128)(2,1)} %v_hbm.1, s32[1,32]{1,0:T(1,128)} %bitcast.21, ...), custom_call_target="tpu_custom_call" | custom-call | tf_op jit(solution)/shard_map/project/pallas_call | solution.py:537
  36.1 56.8 %conditional.1 = ((bf16[32,4096]{1,0:T(8,128)(2,1)S(1)}, f32[1,128]{1,0:T(1,128)S(1)})) conditional(s32[]{:T(128)} %bitcast.6, (bf16[512,128]{1,0:T(8,128)(2,1)S(1)}, f32[256,128]{1,0:T(8,128)S(1)}, bf16[256,512]{1,0:T(8,128)(2,1)S(1)}, f32[8,128]{1,0:T(8,128)S(1)}, f32[128]{0:T(128)}, /*index=5*/bf16[448,4096]{1,0:T(8,128)(2,1)}, ...), branch_computations={%region_0.0_spmd, %region_1.0_spmd} | conditional | bytes 8 | solution.py:640
  36.5 56.4 %feed_forward_256.1 = (bf16[32,4096]{1,0:T(8,128)(2,1)S(1)}, f32[1,128]{1,0:T(1,128)S(1)}) custom-call(bf16[512,128]{1,0:T(8,128)(2,1)S(1)} %get-tuple-element.40.h_ref, f32[256,128]{1,0:T(8,128)S(1)} %get-tuple-element.41.hidden, bf16[256,512]{1,0:T(8,128)(2,1)S(1)} %get-tuple-element.42.back, f32[8,128]{1,0:T(8,128)S(1)} %get-tuple-element.43.table, ...), custom_call_target="tpu_custom_call" | custom-call | tf_op jit(solution)/shard_map/cond/branch_1_fun/feed_forward_256/pallas_call | solution.py:582
  93.0 0.7 copy.27
  93.7 0.5 copy.28

commit v3 on v2

v3 whole, which is shorter than its diff:
```python
import functools
import math
import types

import jax
import jax.numpy as jnp
from jax import lax
from jax.experimental import pallas as pl
from jax.experimental.pallas import tpu as pltpu
from jax.sharding import PartitionSpec as P

HD = 128
EPSILON = 1e-05
MESH = pl.DeviceIdType.MESH
BF = jnp.bfloat16
F32 = jnp.float32
Z_ORDER = (1, 3, 2)
RS_ORDER = (2, 1, 3, 0)


def iota(shape, dim):
    return lax.broadcasted_iota(jnp.int32, shape, dim)


def position():
    return lax.axis_index("attn"), lax.axis_index("ffn"), lax.axis_index("tp")


def remote(src, dst, send, recv, device):
    return pltpu.make_async_remote_copy(
        src_ref=src, dst_ref=dst, send_sem=send, recv_sem=recv, device_id=device, device_id_type=MESH
    )


def greet(devices):
    barrier = pltpu.get_barrier_semaphore()
    for device in devices:
        pl.semaphore_signal(barrier, inc=1, device_id=device, device_id_type=MESH)
    return lambda: pl.semaphore_wait(barrier, len(devices))


def gather_group(buf, half, zs, zr, ys, yr, hs, hr, cs, cr, consume, meanwhile=None):
    a, f, t = position()
    right, left = lax.rem(t + 1, 4), lax.rem(t + 3, 4)
    opposite = lax.rem(t + 2, 4)
    sibling = a + 1 - 2 * lax.rem(a, 2)
    rows = buf.shape[2]
    pieces = (pl.ds(0, half), pl.ds(half, rows - half))
    source = [a] + [lax.rem(a + 8 - 2 * dz, 8) for dz in Z_ORDER]
    sent = []

    def start(copy):
        copy.start()
        sent.append(copy)

    def z_send(k, h):
        piece = buf.at[a, t].at[pieces[h]]
        start(remote(piece, piece, zs.at[k, h], zr.at[k, h], (lax.rem(a + 2 * Z_ORDER[k], 8), f, t)))

    def z_wait(k, h):
        piece = buf.at[source[k + 1], t].at[pieces[h]]
        remote(piece, piece, zs.at[k, h], zr.at[k, h], (a, f, right)).wait_recv()

    def z_forward(h):
        piece = buf.at[source[2 if h else 1], t].at[pieces[h]]
        z = lax.rem(a + (6 if h else 2), 8)
        start(remote(piece, piece, zs.at[2, h], zr.at[2, h], (z, f, t)))

    def y_copy(k, slot, h, way):
        piece = buf.at[source[k], slot].at[pieces[h]]
        return remote(piece, piece, ys.at[k, way, h], yr.at[k, way, h], (a, f, left if way else right))

    def y_send(k, h):
        start(y_copy(k, t, h, h))
        start(y_copy(k, t, h, 1 - h))
        if k == 3:
            piece = buf.at[source[k], t].at[pieces[h]]
            start(remote(piece, piece, hs.at[k, h], hr.at[k, h], (a, f, opposite)))

    def y_forward(k):
        if k == 3:
            return
        for h in range(2):
            slot = right if h else left
            y_copy(k, slot, h, h).wait_recv()
            piece = buf.at[source[k], slot].at[pieces[h]]
            start(remote(piece, piece, hs.at[k, h], hr.at[k, h], (a, f, left if h else right)))

    def core_send(k):
        if k == 3:
            for h in range(2):
                y_copy(k, right if h else left, h, h).wait_recv()
        for h in range(2):
            y_copy(k, left if h else right, h, 1 - h).wait_recv()
        for h in range(2):
            piece = buf.at[source[k], opposite].at[pieces[h]]
            remote(piece, piece, hs.at[k, h], hr.at[k, h], (a, f, right)).wait_recv()
        chunk = buf.at[source[k]]
        start(remote(chunk, chunk, cs.at[k], cr.at[k], (sibling, f, t)))

    def core_wait(k):
        other = source[k] + 1 - 2 * lax.rem(a, 2)
        chunk = buf.at[other]
        remote(chunk, chunk, cs.at[k], cr.at[k], (sibling, f, t)).wait_recv()
        consume(lax.div(source[k], 2))

    z_send(0, 0)
    z_send(1, 1)
    z_send(0, 1)
    z_send(1, 0)
    y_send(0, 0)
    y_send(0, 1)
    if meanwhile is not None:
        sent.extend(meanwhile())
    z_wait(0, 0)
    z_forward(0)
    y_send(1, 0)
    z_wait(1, 1)
    z_forward(1)
    y_send(2, 1)
    z_wait(0, 1)
    y_send(1, 1)
    z_wait(1, 0)
    y_send(2, 0)
    y_forward(0)
    for h in range(2):
        z_wait(2, h)
        y_send(3, h)
    y_forward(1)
    y_forward(2)
    core_send(0)
    core_send(1)
    core_wait(0)
    y_forward(3)
    core_send(2)
    core_wait(1)
    core_send(3)
    core_wait(2)
    core_wait(3)
    return sent


GATHER_SEMS = [
    pltpu.SemaphoreType.DMA((3, 2)),
    pltpu.SemaphoreType.DMA((3, 2)),
    pltpu.SemaphoreType.DMA((4, 2, 2)),
    pltpu.SemaphoreType.DMA((4, 2, 2)),
    pltpu.SemaphoreType.DMA((4, 2)),
    pltpu.SemaphoreType.DMA((4, 2)),
    pltpu.SemaphoreType.DMA((4,)),
    pltpu.SemaphoreType.DMA((4,)),
]


def scatter_group(give, keep, r, settle):
    a, f, t = position()
    right, left, opposite = lax.rem(t + 1, 4), lax.rem(t + 3, 4), lax.rem(t + 2, 4)
    sibling = a + 1 - 2 * lax.rem(a, 2)
    csend, crecv, part, y1s, y1r, y2s, y2r, zsend, zrecv = (
        r.csend, r.crecv, r.part, r.y1s, r.y1r, r.y2s, r.y2r, r.zsend, r.zrecv
    )
    half = part.shape[1] // 2
    halves = (pl.ds(0, half), pl.ds(half, half))
    sent = []

    def start(copy):
        copy.start()
        sent.append(copy)

    def block(i, span, index):
        lanes = pl.ds(pl.multiple_of(index * HD, HD), HD)
        return part[i, span, lanes] + crecv[i, span, lanes].astype(F32)

    def core_copy(i):
        return remote(csend.at[i], crecv.at[i], r.kcs.at[i], r.kcr.at[i], (sibling, f, t))

    def first_copy(i, way, h):
        src, dst = y1s.at[i, way, halves[h]], y1r.at[i, way, halves[h]]
        return remote(src, dst, r.k1s.at[i, way, h], r.k1r.at[i, way, h], (a, f, left if way else right))

    def second_copy(i, way):
        device = (a, f, left if way else right)
        return remote(y2s.at[i, way], y2r.at[i, way], r.k2s.at[i, way], r.k2r.at[i, way], device)

    def z_copy(i, h):
        src, dst = zsend.at[i, halves[h]], zrecv.at[i, halves[h]]
        return remote(src, dst, r.kzs.at[i, h], r.kzr.at[i, h], (lax.rem(a + 2 * RS_ORDER[i], 8), f, t))

    def core_give(i):
        give(i)
        start(core_copy(i))
        keep(i)

    def y_first(i):
        core_copy(i).wait_recv()
        for way in range(2):
            y1s[i, way, halves[way], :] = block(i, halves[way], opposite).astype(BF)
            start(first_copy(i, way, way))
        for way in range(2):
            span = halves[1 - way]
            y1s[i, way, span, :] = block(i, span, left if way else right).astype(BF)
            start(first_copy(i, way, 1 - way))

    def y_second(i):
        for way in range(2):
            value = block(i, halves[way], left if way else right)
            first_copy(i, way, way).wait_recv()
            y2s[i, way] = (value + y1r[i, way, halves[way], :].astype(F32)).astype(BF)
            start(second_copy(i, way))

    def y_sum(i, h):
        value = block(i, halves[h], t)
        first_copy(i, 1 - h, h).wait_recv()
        value = value + y1r[i, 1 - h, halves[h], :].astype(F32)
        second_copy(i, h).wait_recv()
        return value + y2r[i, h].astype(F32)

    def z_give(i):
        for h in range(2):
            zsend[i, halves[h], :] = y_sum(i, h).astype(BF)
            start(z_copy(i, h))

    core_give(0)
    core_give(1)
    y_first(0)
    core_give(2)
    y_first(1)
    y_second(0)
    core_give(3)
    y_first(2)
    y_second(1)
    y_first(3)
    settle()
    z_give(0)
    y_second(2)
    z_give(1)
    y_second(3)
    z_give(2)
    total = []
    for h in range(2):
        value = y_sum(3, h)
        for i in range(3):
            z_copy(i, h).wait_recv()
            value = value + zrecv[i, halves[h], :].astype(F32)
        total.append(value)
    return jnp.concatenate(total, axis=0), sent


def attend(q, k, v, lens, att):
    for part in range(2):
        base = part * 16
        heads = jnp.concatenate([q[base : base + 16, h * HD : (h + 1) * HD] for h in range(8)], axis=0)
        slot = lax.rem(iota((128, 128), 0), 16)
        scores = jnp.zeros((128, 128), F32)
        for pair in range(8):
            block = k[base + 2 * pair : base + 2 * pair + 2].reshape(256, HD)
            both = lax.dot_general(heads, block, (((1,), (1,)), ((), ())), preferred_element_type=F32)
            scores = jnp.where(slot == 2 * pair, both[:, :128], scores)
            scores = jnp.where(slot == 2 * pair + 1, both[:, 128:], scores)
        scores = scores / math.sqrt(HD)
        limit = jnp.concatenate([lens[base : base + 16, :]] * 8, axis=0)
        valid = iota((128, 128), 1) < limit
        top = jnp.max(jnp.where(valid, scores, -1e30), axis=-1, keepdims=True)
        unnormed = jnp.where(valid, jnp.exp(scores - top), 0.0)
        summed = jnp.maximum(jnp.sum(unnormed, axis=-1, keepdims=True), 1.0)
        weights = unnormed / summed
        total = jnp.zeros((128, HD), F32)
        for pair in range(8):
            block = v[base + 2 * pair : base + 2 * pair + 2].reshape(256, HD)
            masked = jnp.concatenate(
                [jnp.where(slot == 2 * pair, weights, 0.0), jnp.where(slot == 2 * pair + 1, weights, 0.0)], axis=1
            ).astype(BF)
            total = total + jnp.dot(masked, block, preferred_element_type=F32)
        total = total.astype(BF)
        for h in range(8):
            att[pl.ds(base, 16), pl.ds(h * HD, HD)] = total[h * 16 : (h + 1) * 16, :]


def project_part(r, peers):
    a, f, t = position()
    q, k, v, wout, lens, routes, wide, codes, buf, res = (
        r.q, r.k, r.v, r.wout, r.lens, r.routes, r.wide, r.codes, r.heads, r.res
    )
    cbuf, place, sbuf, hbuf, tsend, tbuf = r.cbuf, r.place, r.sbuf, r.hbuf, r.tsend, r.tbuf
    in_sems, rs, rr, es, er, fs, fr, gs, gr = r.in_sems, r.rs, r.rr, r.es, r.er, r.fs, r.fr, r.gs, r.gr
    back_out, res_hbm, hsend, hall = r.back, r.res_hbm, r.hsend, r.hall
    own_z, core = lax.div(a, 2), lax.rem(a, 2)
    attn_peers = [lax.rem(a + step, 8) for step in range(1, 8)]
    ffn_peers = [lax.rem(f + step, 8) for step in range(1, 8)]
    all_here = greet(peers)
    loads = []
    pairs = (
        (r.len_hbm, lens), (r.route_hbm, routes), (r.q_hbm, q), (r.k_hbm, k), (r.v_hbm, v), (r.wout_hbm, wout),
    )
    for i, (src, dst) in enumerate(pairs):
        copy = pltpu.make_async_copy(src, dst, in_sems.at[i])
        copy.start()
        loads.append(copy)

    def columns(index):
        return pl.ds(pl.multiple_of((index * 4 + t) * HD, HD), HD)

    loads[0].wait()
    loads[1].wait()
    wide[...] = jnp.zeros((8, 128), F32)
    wide[0:1, 0:32] = lens[...].astype(F32)
    wide[1:2, 0:32] = jnp.where(lens[...] > 0, routes[...], 8).astype(F32) + 1.0
    limits = jnp.broadcast_to(wide[0:1, :], (128, 128)).T[:32].astype(jnp.int32)
    tile = jnp.where(iota((128, 256), 0) == lax.rem(iota((128, 256), 1), 32), 1.0, 0.0).astype(BF)
    tiled = jnp.dot(jnp.broadcast_to(wide[1:2, :], (16, 128)).astype(BF), tile, preferred_element_type=F32)
    codes[...] = jnp.where(iota((1, 256), 1) // 32 == a, tiled[:1], 0.0)
    for copy in loads[2:5]:
        copy.wait()
    attend(q, k, v, limits, buf.at[a, t])
    cbuf[a] = codes[...]
    own = pltpu.make_async_copy(res_hbm.at[:, columns(a)], res.at[a], r.own_sem)
    own.start()
    all_here()

    def exchange():
        sent = []
        for i, peer in enumerate(attn_peers):
            copy = remote(codes, cbuf.at[a], es.at[i], er.at[i], (peer, f, t))
            copy.start()
            sent.append(copy)
            copy = remote(res_hbm.at[:, columns(peer)], res.at[a], rs.at[i], rr.at[i], (peer, f, t))
            copy.start()
            sent.append(copy)
        return sent

    def prepare():
        loads[5].wait()
        own.wait()
        for i in range(7):
            peer = lax.rem(a + 7 - i, 8)
            remote(cbuf.at[peer], cbuf.at[peer], es.at[i], er.at[i], (peer, f, t)).wait_recv()
        code = cbuf[0]
        for i in range(1, 8):
            code = code + cbuf[i]
        code = code - 1.0
        code_t = jnp.broadcast_to(code, (256, 256)).T
        down, across = iota((256, 256), 0), iota((256, 256), 1)
        same = (code_t == code) & (down // 32 == across // 32)
        rank_row = jnp.sum(jnp.where(same & (down < across), 1.0, 0.0), axis=0, keepdims=True)
        rank_col = jnp.sum(jnp.where(same & (across < down), 1.0, 0.0), axis=1, keepdims=True)
        target_row = (code * 8.0 + rank_row).astype(jnp.int32)
        target_col = (code_t[:, 0:1] * 8.0 + rank_col).astype(jnp.int32)
        p, q_index = iota((512, 64), 0), iota((512, 64), 1)
        wanted = (lax.rem(p, 128) // 16) * 8 + lax.rem(p, 8)
        of_z = jnp.concatenate(
            [jnp.broadcast_to(target_row[:, z * 64 : (z + 1) * 64], (128, 64)) for z in range(4)], axis=0
        )
        hit = (wanted == of_z) & (lax.rem(p // 8, 2) == q_index // 32)
        place[...] = jnp.where(hit, 1.0, 0.0).astype(BF).reshape(4, 128, 64)
        r.targets[...] = jnp.broadcast_to(target_col, (256, 128))
        own_targets = r.targets[pl.ds(pl.multiple_of(own_z * 64, 64), 64), :]
        q_index, p = iota((64, 128), 0), iota((64, 128), 1)
        hit = ((p // 16) * 8 + lax.rem(p, 8) == own_targets) & (lax.rem(p // 8, 2) == q_index // 32)
        back_out[...] = jnp.where(hit, 1.0, 0.0).astype(BF)
        q_index, j = iota((256, 128), 0), iota((256, 128), 1)
        block = (q_index // 32 == lax.rem(j, 8)) & (j < 64)
        named = (code_t[:, :128] == (j // 8).astype(F32)) & block
        tsend[...] = jnp.sum(jnp.where(named, 1.0, 0.0), axis=0, keepdims=True)
        tbuf[f] = tsend[...]
        for i in range(7):
            peer = lax.rem(a + 7 - i, 8)
            remote(res.at[peer], res.at[peer], rs.at[i], rr.at[i], (peer, f, t)).wait_recv()

    later = []
    chunks = []

    def consume(z):
        if not chunks:
            prepare()
            for i, peer in enumerate(ffn_peers):
                copy = remote(tsend, tbuf.at[f], gs.at[i], gr.at[i], (a, peer, t))
                copy.start()
                later.append(copy)
        number = len(chunks)
        chunks.append(z)
        pair = pl.ds(2 * z, 2)
        total = jnp.zeros((64, HD), F32)
        for other in range(4):
            left = buf[pair, other].reshape(64, 1024)
            total = total + jnp.dot(left, wout[pl.ds(other * 1024, 1024), :], preferred_element_type=F32)
        total = total + res[pair].reshape(64, HD).astype(F32)
        if number:
            hsend[z] = total
        else:
            hall[z] = total
        routed = jnp.dot(place[z], total.astype(BF), preferred_element_type=F32).astype(BF)
        sbuf[z] = routed.reshape(8, 16, HD)
        for i, peer in enumerate(ffn_peers):
            copy = remote(sbuf.at[z, peer], hbuf.at[f, z], fs.at[number, i], fr.at[number, i], (a, peer, t))
            copy.start()
            later.append(copy)
        hbuf[f, z] = sbuf[z, f]
        if number:
            copy = remote(hsend.at[z], hall.at[own_z], r.vs.at[number], r.vr.at[number], (z * 2 + core, f, t))
            copy.start()
            later.append(copy)

    sent = gather_group(buf, 16, *r.heads_sems, consume, exchange)
    for i in range(7):
        peer = lax.rem(f + 7 - i, 8)
        remote(tbuf.at[peer], tbuf.at[peer], gs.at[i], gr.at[i], (a, peer, t)).wait_recv()
    table = tbuf[...].reshape(8, 128)
    r.table[...] = table
    sums = jnp.broadcast_to(jnp.sum(table, axis=0, keepdims=True), (16, 128)).astype(BF)
    fold = jnp.where(iota((128, 128), 0) // 8 == iota((128, 128), 1), 1.0, 0.0).astype(BF)
    totals = jnp.dot(sums, fold, preferred_element_type=F32)
    r.small[0, 0] = jnp.where(jnp.max(totals) <= float(COMMON), 1, 0)
    positions(COMMON, r)
    for number, z in enumerate(chunks):
        for i in range(7):
            peer = lax.rem(f + 7 - i, 8)
            slot = hbuf.at[peer, z]
            remote(slot, slot, fs.at[number, i], fr.at[number, i], (a, peer, t)).wait_recv()
    r.h[...] = hbuf[...].reshape(512, HD)

    def finish():
        for i, dz in enumerate(Z_ORDER):
            slot = hall.at[lax.rem(own_z + dz, 4)]
            remote(slot, slot, r.vs.at[i + 1], r.vr.at[i + 1], (lax.rem(a + 2 * dz, 8), f, t)).wait_recv()
        r.hidden[...] = hall[...].reshape(256, HD)

    return sent + later, finish


def start_weights(r):
    loads = []
    for i, (src, dst) in enumerate(((r.wg_hbm, r.wg), (r.wu_hbm, r.wu), (r.wd_hbm, r.wd))):
        copy = pltpu.make_async_copy(src, dst, r.weight_sems.at[i])
        copy.start()
        loads.append(copy)
    return loads


def positions(rows, r):
    f = lax.axis_index("ffn")
    j, p = iota((128, 512), 0), iota((128, 512), 1)
    pick = jnp.where(j == f * 8 + lax.rem(p // 8, 8), 1.0, 0.0).astype(BF)
    table16 = jnp.concatenate([r.table[...], r.table[...]], axis=0).astype(BF)
    counts = jnp.dot(table16, pick, preferred_element_type=F32)[:8]
    s, p = iota((8, 512), 0), iota((8, 512), 1)
    counts = jnp.sum(jnp.where(s == p // 64, counts, 0.0), axis=0, keepdims=True)
    live = lax.rem(iota((1, 512), 1), 8).astype(F32) < counts
    flags = jnp.broadcast_to(jnp.where(live, 1.0, 0.0), (16, 512)).astype(BF)
    before = jnp.where(iota((512, 512), 0) < iota((512, 512), 1), 1.0, 0.0).astype(BF)
    place = jnp.dot(flags, before, preferred_element_type=F32)[:1]
    place = jnp.where(live, place, -1.0)
    r.compact[...] = jnp.where(iota((rows, 512), 0) == place.astype(jnp.int32), 1.0, 0.0).astype(BF)
    place_t = jnp.broadcast_to(place, (128, 512)).T.astype(jnp.int32)
    for i in range(rows // 128):
        hit = place_t == iota((512, 128), 1) + i * 128
        r.unplace[:, pl.ds(i * 128, 128)] = jnp.where(hit, 1.0, 0.0).astype(BF)


def ffn_part(rows, r, loads, pending, all_here, met, finish):
    a, f, t = position()
    hidden, back, gain, stream_out, sums_out = r.hidden, r.back, r.gain, r.stream, r.sums
    wg, wu, wd, buf, gate, up, act = r.wg, r.wu, r.wd, r.buf, r.gate, r.up, r.act
    csend, part, unplace, rsend, rbuf, final, line = r.csend, r.part, r.unplace, r.rsend, r.rbuf, r.final, r.line
    kbs, kbr, kys, kyr = r.kbs, r.kbr, r.kys, r.kyr
    z, core = lax.div(a, 2), lax.rem(a, 2)
    right, left, opposite = lax.rem(t + 1, 4), lax.rem(t + 3, 4), lax.rem(t + 2, 4)
    sibling = a + 1 - 2 * core
    half = rows // 2
    blocks = rows // 128
    attn_peers = [lax.rem(a + step, 8) for step in range(1, 8)]
    ffn_peers = [lax.rem(f + step, 8) for step in range(1, 8)]
    tp_peers = [lax.rem(t + step, 4) for step in range(1, 4)]

    picked = jnp.dot(r.compact[...], r.h[...], preferred_element_type=F32)
    slot = buf.at[a, t]
    slot[pl.ds(0, rows), :] = (picked * gain[...]).astype(BF)
    squares = picked * picked
    tail = jnp.zeros((16, 128), F32)
    line_index = iota((16, 128), 0)
    for i in range(blocks):
        block = jnp.sum(squares[i * 128 : (i + 1) * 128].T, axis=0, keepdims=True)
        high = block.astype(BF).astype(F32)
        tail = jnp.where(line_index == i, high, tail)
        tail = jnp.where(line_index == blocks + i, block - high, tail)
    slot[pl.ds(rows, 16), :] = tail.astype(BF)

    all_here()

    first = [True]

    def consume(chunk):
        if first[0]:
            loads[0].wait()
            loads[1].wait()
        for c in range(2):
            index = chunk * 2 + c
            depth = pl.ds(pl.multiple_of(index * 512, 512), 512)
            for m in range(0, rows, 256):
                span = pl.ds(m, 256)
                lhs = jnp.concatenate([buf[index, other, span, :] for other in range(4)], axis=1)
                for weight, total in ((wg, gate), (wu, up)):
                    value = lax.dot_general(
                        lhs, weight[:, depth], (((1,), (1,)), ((), ())), preferred_element_type=F32
                    )
                    if first[0] and c == 0:
                        total[span, :] = value
                    else:
                        total[span, :] += value
        first[0] = False

    def settle():
        for copy in pending:
            copy.wait_send()
        return []

    gathered = gather_group(buf, half + 16, *r.normed_sems, consume, settle)
    met()
    sent = []

    tails = jnp.sum(buf[:, :, pl.ds(rows, 16), :].astype(F32).reshape(32, 16, 128), axis=0)
    for i in range(blocks):
        span = pl.ds(i * 128, 128)
        total = tails[i : i + 1] + tails[blocks + i : blocks + i + 1]
        inverse = lax.rsqrt(total / 4096.0 + EPSILON)
        scale = jnp.broadcast_to(inverse, (128, 128)).T
        scale = jnp.concatenate([scale] * 4, axis=1)[:, :448]
        g = gate[span, :] * scale
        act[span, :] = (g / (1.0 + jnp.exp(-g)) * (up[span, :] * scale)).astype(BF)
    loads[2].wait()

    def chunk_columns(dz, c):
        index = lax.rem(z + dz, 4) * 2 + c
        return pl.ds(pl.multiple_of(index * 512, 512), 512)

    def down(dz, c, store):
        for m in range(0, rows, 256):
            span = pl.ds(m, 256)
            store(span, jnp.dot(act[span, :], wd[:, chunk_columns(dz, c)], preferred_element_type=F32))

    def give(i):
        def store(span, value):
            csend[i, span, :] = value.astype(BF)

        down(RS_ORDER[i], 1 - core, store)

    def keep(i):
        def store(span, value):
            part[i, span, :] = value

        down(RS_ORDER[i], core, store)

    def settle_gather():
        for copy in gathered:
            copy.wait_send()

    total, scattered = scatter_group(give, keep, r, settle_gather)
    sums_out[...] = jnp.sum(total, axis=0, keepdims=True)
    spread = jnp.dot(unplace[...], total.astype(BF), preferred_element_type=F32).astype(BF)
    rsend[...] = spread.reshape(8, 4, 16, HD)
    finish()

    def start(copy):
        copy.start()
        sent.append(copy)

    for dz in (2, 1, 3, 0):
        for step in range(8):
            if dz or step:
                to_z, to_f = lax.rem(z + dz, 4), lax.rem(f + step, 8)
                src, dst = rsend.at[to_f, to_z], rbuf.at[z, f]
                start(remote(src, dst, kbs.at[dz, step], kbr.at[dz, step], (to_z * 2 + core, to_f, t)))
    rbuf[z, f] = rsend[f, z]
    for copy in scattered:
        copy.wait_send()
    placing = back[...]
    live_rows = jnp.sum(placing.astype(F32), axis=1, keepdims=True) > 0.5

    def last_copy(dz, from_z, cross, step):
        index = from_z * 2 + core
        src, dst = line.at[from_z, 1 - core if cross else core], final.at[t, index]
        device = (sibling if cross else a, f, lax.rem(t + step, 4))
        return remote(src, dst, kys.at[dz, cross, step], kyr.at[dz, cross, step], device)

    for dz in (0, 1, 3, 2):
        from_z = lax.rem(z + 4 - dz, 4)
        for step in range(8):
            if dz or step:
                slot = rbuf.at[from_z, lax.rem(f + 8 - step, 8)]
                remote(slot, slot, kbs.at[dz, step], kbr.at[dz, step], (sibling, f, t)).wait_recv()
        value = jnp.dot(placing, rbuf[from_z].reshape(128, HD), preferred_element_type=F32)
        value = value + hidden[pl.ds(pl.multiple_of(from_z * 64, 64), 64), :]
        line[from_z] = jnp.where(live_rows, value, 0.0).astype(BF).reshape(2, 32, HD)
        for step in (2, 1, 3):
            start(last_copy(dz, from_z, 0, step))
            start(last_copy(dz, from_z, 1, step))
        start(last_copy(dz, from_z, 1, 0))
        final[t, from_z * 2 + core] = line[from_z, core]
    for dz in (0, 1, 3, 2):
        from_z = lax.rem(z + 4 - dz, 4)
        for cross in range(2):
            for step in range(4):
                if cross or step:
                    slot = final.at[lax.rem(t + 4 - step, 4), from_z * 2 + (1 - core if cross else core)]
                    remote(slot, slot, kys.at[dz, cross, step], kyr.at[dz, cross, step], (sibling, f, t)).wait_recv()
    for other in range(4):
        for source in range(8):
            stream_out[:, pl.ds((source * 4 + other) * HD, HD)] = final[other, source]
    for copy in sent:
        copy.wait_send()


VMEM = pl.BlockSpec(memory_space=pltpu.VMEM)
ANY = pl.BlockSpec(memory_space=pl.ANY)
DMA = pltpu.SemaphoreType.DMA
COMMON = 256

PROJECT_SCRATCH = [
    ("q", pltpu.VMEM((32, 1024), BF)),
    ("k", pltpu.VMEM((32, 128, HD), BF)),
    ("v", pltpu.VMEM((32, 128, HD), BF)),
    ("wout", pltpu.VMEM((4096, HD), BF)),
    ("lens", pltpu.VMEM((1, 32), jnp.int32)),
    ("routes", pltpu.VMEM((1, 32), jnp.int32)),
    ("wide", pltpu.VMEM((8, 128), F32)),
    ("codes", pltpu.VMEM((1, 256), F32)),
    ("heads", pltpu.VMEM((8, 4, 32, 1024), BF)),
    ("res", pltpu.VMEM((8, 32, HD), BF)),
    ("cbuf", pltpu.VMEM((8, 1, 256), F32)),
    ("place", pltpu.VMEM((4, 128, 64), BF)),
    ("sbuf", pltpu.VMEM((4, 8, 16, HD), BF)),
    ("hbuf", pltpu.VMEM((8, 4, 16, HD), BF)),
    ("tsend", pltpu.VMEM((1, 128), F32)),
    ("tbuf", pltpu.VMEM((8, 1, 128), F32)),
    ("in_sems", DMA((6,))),
    *[(name, DMA((7,))) for name in ("rs", "rr", "es", "er", "gs", "gr")],
    ("fs", DMA((4, 7))),
    ("fr", DMA((4, 7))),
    ("own_sem", DMA(())),
    ("targets", pltpu.VMEM((256, 128), jnp.int32)),
    ("hsend", pltpu.VMEM((4, 64, HD), F32)),
    ("hall", pltpu.VMEM((4, 64, HD), F32)),
    ("vs", DMA((4,))),
    ("vr", DMA((4,))),
]


def ffn_scratch(rows):
    return [
        ("wg", pltpu.VMEM((448, 4096), BF)),
        ("wu", pltpu.VMEM((448, 4096), BF)),
        ("wd", pltpu.VMEM((448, 4096), BF)),
        ("compact", pltpu.VMEM((rows, 512), BF)),
        ("buf", pltpu.VMEM((8, 4, rows + 16, HD), BF)),
        ("gate", pltpu.VMEM((rows, 448), F32)),
        ("up", pltpu.VMEM((rows, 448), F32)),
        ("act", pltpu.VMEM((rows, 448), BF)),
        ("csend", pltpu.VMEM((4, rows, 512), BF)),
        ("crecv", pltpu.VMEM((4, rows, 512), BF)),
        ("part", pltpu.VMEM((4, rows, 512), F32)),
        ("y1s", pltpu.VMEM((4, 2, rows, HD), BF)),
        ("y1r", pltpu.VMEM((4, 2, rows, HD), BF)),
        ("y2s", pltpu.VMEM((4, 2, rows // 2, HD), BF)),
        ("y2r", pltpu.VMEM((4, 2, rows // 2, HD), BF)),
        ("zsend", pltpu.VMEM((3, rows, HD), BF)),
        ("zrecv", pltpu.VMEM((3, rows, HD), BF)),
        ("unplace", pltpu.VMEM((512, rows), BF)),
        ("rsend", pltpu.VMEM((8, 4, 16, HD), BF)),
        ("rbuf", pltpu.VMEM((4, 8, 16, HD), BF)),
        ("final", pltpu.VMEM((4, 8, 32, HD), BF)),
        ("line", pltpu.VMEM((4, 2, 32, HD), BF)),
        ("weight_sems", DMA((3,))),
        ("kcs", DMA((4,))),
        ("kcr", DMA((4,))),
        *[(name, DMA((4, 2, 2))) for name in ("k1s", "k1r")],
        *[(name, DMA((4, 2))) for name in ("k2s", "k2r")],
        *[(name, DMA((3, 2))) for name in ("kzs", "kzr")],
        *[(name, DMA((4, 8))) for name in ("kbs", "kbr")],
        *[(name, DMA((4, 2, 4))) for name in ("kys", "kyr")],
    ]


def peers_of():
    a, f, t = position()
    return (
        [(lax.rem(a + step, 8), f, t) for step in range(1, 8)]
        + [(a, lax.rem(f + step, 8), t) for step in range(1, 8)]
        + [(a, f, lax.rem(t + step, 4)) for step in range(1, 4)]
    )


def call(body, name, identity, inputs, outputs, scratch, gathers, operands):
    names = [n for n, _ in inputs] + [n for n, _, _ in outputs] + [n for n, _ in scratch]
    count = len(GATHER_SEMS)

    def kernel(*refs):
        r = types.SimpleNamespace(**dict(zip(names, refs)))
        for i, gather in enumerate(gathers):
            start = len(names) + i * count
            setattr(r, gather, refs[start : start + count])
        body(r)

    return pl.pallas_call(
        kernel,
        name=name,
        out_shape=tuple(shape for _, shape, _ in outputs),
        in_specs=[spec for _, spec in inputs],
        out_specs=[spec for _, _, spec in outputs],
        scratch_shapes=[spec for _, spec in scratch] + GATHER_SEMS * len(gathers),
        compiler_params=pltpu.CompilerParams(
            collective_id=identity, has_side_effects=True, vmem_limit_bytes=63 * 2**20
        ),
    )(*operands)


RESULTS = [
    ("stream", jax.ShapeDtypeStruct((32, 4096), BF), VMEM),
    ("sums", jax.ShapeDtypeStruct((1, HD), F32), VMEM),
]
ROUTED = [
    ("h", jax.ShapeDtypeStruct((512, HD), BF), VMEM),
    ("hidden", jax.ShapeDtypeStruct((256, HD), F32), VMEM),
    ("back", jax.ShapeDtypeStruct((64, 128), BF), VMEM),
    ("table", jax.ShapeDtypeStruct((8, 128), F32), VMEM),
]
WEIGHTS = [("gain", VMEM), ("wg_hbm", ANY), ("wu_hbm", ANY), ("wd_hbm", ANY)]


def layer(*operands):
    def body(r):
        peers = peers_of()
        loads = start_weights(r)
        pending, finish = project_part(r, peers)
        ffn_part(COMMON, r, loads, pending, lambda: None, lambda: None, finish)

    inputs = [
        (name, ANY)
        for name in ("q_hbm", "k_hbm", "v_hbm", "len_hbm", "route_hbm", "res_hbm", "wout_hbm")
    ] + WEIGHTS
    outputs = RESULTS + ROUTED + [
        ("small", jax.ShapeDtypeStruct((1, 1), jnp.int32), pl.BlockSpec(memory_space=pltpu.SMEM))
    ]
    scratch = PROJECT_SCRATCH + ffn_scratch(COMMON)
    return call(body, "layer", 0, inputs, outputs, scratch, ["heads_sems", "normed_sems"], operands)


def feed_forward(rows, identity, *operands):
    def body(r):
        all_here = greet(peers_of())
        loads = start_weights(r)
        positions(rows, r)
        a, f, t = position()

        def meet():
            for step in range(1, 8):
                peer = (a, lax.rem(f + step, 8), t)
                pl.semaphore_signal(r.met, inc=1, device_id=peer, device_id_type=MESH)

        ffn_part(rows, r, loads, [], all_here, meet, lambda: pl.semaphore_wait(r.met, 7))

    inputs = [(name, VMEM) for name, _, _ in ROUTED] + WEIGHTS
    scratch = ffn_scratch(rows) + [("met", pltpu.SemaphoreType.REGULAR)]
    return call(body, "feed_forward", identity, inputs, RESULTS, scratch, ["normed_sems"], operands)


def per_device(
    queries, keys, values, lengths, routes, residual, w_out, norm_gain, w_gate, w_up, w_down
):
    weights = (norm_gain[None, :], w_gate[0].T, w_up[0].T, w_down[0])
    stream, sums, h, hidden, back, table, small = layer(
        queries, keys, values, lengths.reshape(1, 32), routes.reshape(1, 32), residual, w_out, *weights
    )
    return lax.cond(
        small[0, 0] == 1,
        lambda *operands: (stream, sums),
        functools.partial(feed_forward, 512, 1),
        h, hidden, back, table, *weights,
    )


def solution(mesh):
    placed = (
        P(("attn", "ffn"), "tp"),
        P(("attn", "ffn"), None, "tp"),
        P(("attn", "ffn"), None, "tp"),
        P(("attn", "ffn")),
        P(("attn", "ffn"), None),
        P(("attn", "ffn"), None),
        P(None, ("attn", "tp")),
        P(("attn", "tp")),
        P("ffn", None, ("attn", "tp")),
        P("ffn", None, ("attn", "tp")),
        P("ffn", ("attn", "tp"), None),
    )
    return jax.shard_map(
        per_device,
        mesh=mesh,
        in_specs=placed,
        out_specs=(P(("attn", "ffn"), None), P("ffn", ("attn", "tp"))),
        check_vma=False,
    )
```

time: 94.3 us -> 90.6 us (0.961)
  Pallas kernels: 91.3 us -> 87.8 us
    pallas_call x2 -> x1, Pallas kernels: 91.3 us -> 87.8 us  [call(): pl.pallas_call(kernel, name=name, out_shape=tuple((shape for _, shape, _...]
where the time goes in v3:
time: 90.6 us; the launch traced here: 90.5 us
  Pallas kernels  87.8 us (97%)
  between operations  1.28 us (1%)
  local copies, waits for them, and re-layouts  1.22 us (1%)
    pallas_call x1, Pallas kernels, call(): pl.pallas_call(kernel, name=name, out_shape=tuple((shape for _, shape, _...  87.8 us

profile of v3, /device:TPU:1, one launch (start us, length us, event | category | flops | bytes accessed | tf_op | source)
XLA Modules:
  0.0 90.5 jit_solution(11374590346036701161)
XLA Ops:
  0.6 0.0 copy-start
  0.6 87.8 %layer.1 = (bf16[32,4096]{1,0:T(8,128)(2,1)S(1)}, f32[1,128]{1,0:T(1,128)S(1)}, bf16[512,128]{1,0:T(8,128)(2,1)S(1)}, f32[256,128]{1,0:T(8,128)S(1)}, bf16[64,12...) custom-call(bf16[32,1024]{1,0:T(8,128)(2,1)} %refs_0_.1, bf16[32,128,128]{2,1,0:T(8,128)(2,1)} %refs_1_.1, ...), custom_call_target="tpu_custom_call" | custom-call | tf_op jit(solution)/shard_map/layer/pallas_call | solution.py:702
  89.1 0.0 copy-done
  89.1 0.2 conditional.1
  89.3 0.7 copy.23
  90.0 0.5 copy.24
Async XLA Ops:
  0.6 88.5 %copy-start = (f32[128]{0:T(128)S(1)}, f32[128]{0:T(128)}, u32[]{:S(2)}) copy-start(f32[128]{0:T(128)} %param.20) | copy-start | bytes 1540

commit v4 on v3

--- a/solution.py
+++ b/solution.py
@@ -16,6 +16,10 @@
 F32 = jnp.float32
 Z_ORDER = (1, 3, 2)
 RS_ORDER = (2, 1, 3, 0)
+
+
+def upper_half(rows):
+    return (rows // 16 + 1) // 2 * 16
 
 
 def iota(shape, dim):
@@ -159,8 +163,10 @@
     csend, crecv, part, y1s, y1r, y2s, y2r, zsend, zrecv = (
         r.csend, r.crecv, r.part, r.y1s, r.y1r, r.y2s, r.y2r, r.zsend, r.zrecv
     )
-    half = part.shape[1] // 2
-    halves = (pl.ds(0, half), pl.ds(half, half))
+    half = upper_half(part.shape[1])
+    sizes = (half, part.shape[1] - half)
+    halves = (pl.ds(0, sizes[0]), pl.ds(half, sizes[1]))
+    starts = (pl.ds(0, sizes[0]), pl.ds(0, sizes[1]))
     sent = []
 
     def start(copy):
@@ -180,7 +186,8 @@
 
     def second_copy(i, way):
         device = (a, f, left if way else right)
-        return remote(y2s.at[i, way], y2r.at[i, way], r.k2s.at[i, way], r.k2r.at[i, way], device)
+        src, dst = y2s.at[i, way, starts[way]], y2r.at[i, way, starts[way]]
+        return remote(src, dst, r.k2s.at[i, way], r.k2r.at[i, way], device)
 
     def z_copy(i, h):
         src, dst = zsend.at[i, halves[h]], zrecv.at[i, halves[h]]
@@ -205,7 +212,7 @@
         for way in range(2):
             value = block(i, halves[way], left if way else right)
             first_copy(i, way, way).wait_recv()
-            y2s[i, way] = (value + y1r[i, way, halves[way], :].astype(F32)).astype(BF)
+            y2s[i, way, starts[way], :] = (value + y1r[i, way, halves[way], :].astype(F32)).astype(BF)
             start(second_copy(i, way))
 
     def y_sum(i, h):
@@ -213,7 +220,7 @@
         first_copy(i, 1 - h, h).wait_recv()
         value = value + y1r[i, 1 - h, halves[h], :].astype(F32)
         second_copy(i, h).wait_recv()
-        return value + y2r[i, h].astype(F32)
+        return value + y2r[i, h, starts[h], :].astype(F32)
 
     def z_give(i):
         for h in range(2):
@@ -451,7 +458,7 @@
     place = jnp.where(live, place, -1.0)
     r.compact[...] = jnp.where(iota((rows, 512), 0) == place.astype(jnp.int32), 1.0, 0.0).astype(BF)
     place_t = jnp.broadcast_to(place, (128, 512)).T.astype(jnp.int32)
-    for i in range(rows // 128):
+    for i in range(-(-rows // 128)):
         hit = place_t == iota((512, 128), 1) + i * 128
         r.unplace[:, pl.ds(i * 128, 128)] = jnp.where(hit, 1.0, 0.0).astype(BF)
 
@@ -465,8 +472,13 @@
     z, core = lax.div(a, 2), lax.rem(a, 2)
     right, left, opposite = lax.rem(t + 1, 4), lax.rem(t + 3, 4), lax.rem(t + 2, 4)
     sibling = a + 1 - 2 * core
-    half = rows // 2
-    blocks = rows // 128
+    blocks = -(-rows // 128)
+    padding = jnp.zeros((blocks * 128 - rows, HD), F32)
+    tiles = [pl.ds(0, rows)] if rows < 384 else [pl.ds(m, 256) for m in range(0, rows, 256)]
+
+    def padded(value):
+        return jnp.concatenate([value, padding], axis=0) if blocks * 128 > rows else value
+
     attn_peers = [lax.rem(a + step, 8) for step in range(1, 8)]
     ffn_peers = [lax.rem(f + step, 8) for step in range(1, 8)]
     tp_peers = [lax.rem(t + step, 4) for step in range(1, 4)]
@@ -474,7 +486,7 @@
     picked = jnp.dot(r.compact[...], r.h[...], preferred_element_type=F32)
     slot = buf.at[a, t]
     slot[pl.ds(0, rows), :] = (picked * gain[...]).astype(BF)
-    squares = picked * picked
+    squares = padded(picked * picked)
     tail = jnp.zeros((16, 128), F32)
     line_index = iota((16, 128), 0)
     for i in range(blocks):
@@ -495,8 +507,7 @@
         for c in range(2):
             index = chunk * 2 + c
             depth = pl.ds(pl.multiple_of(index * 512, 512), 512)
-            for m in range(0, rows, 256):
-                span = pl.ds(m, 256)
+            for span in tiles:
                 lhs = jnp.concatenate([buf[index, other, span, :] for other in range(4)], axis=1)
                 for weight, total in ((wg, gate), (wu, up)):
                     value = lax.dot_general(
@@ -513,17 +524,18 @@
             copy.wait_send()
         return []
 
-    gathered = gather_group(buf, half + 16, *r.normed_sems, consume, settle)
+    gathered = gather_group(buf, upper_half(rows + 16), *r.normed_sems, consume, settle)
     met()
     sent = []
 
     tails = jnp.sum(buf[:, :, pl.ds(rows, 16), :].astype(F32).reshape(32, 16, 128), axis=0)
     for i in range(blocks):
-        span = pl.ds(i * 128, 128)
+        size = min(128, rows - i * 128)
+        span = pl.ds(i * 128, size)
         total = tails[i : i + 1] + tails[blocks + i : blocks + i + 1]
         inverse = lax.rsqrt(total / 4096.0 + EPSILON)
         scale = jnp.broadcast_to(inverse, (128, 128)).T
-        scale = jnp.concatenate([scale] * 4, axis=1)[:, :448]
+        scale = jnp.concatenate([scale] * 4, axis=1)[:size, :448]
         g = gate[span, :] * scale
         act[span, :] = (g / (1.0 + jnp.exp(-g)) * (up[span, :] * scale)).astype(BF)
     loads[2].wait()
@@ -533,8 +545,7 @@
         return pl.ds(pl.multiple_of(index * 512, 512), 512)
 
     def down(dz, c, store):
-        for m in range(0, rows, 256):
-            span = pl.ds(m, 256)
+        for span in tiles:
             store(span, jnp.dot(act[span, :], wd[:, chunk_columns(dz, c)], preferred_element_type=F32))
 
     def give(i):
@@ -555,7 +566,7 @@
 
     total, scattered = scatter_group(give, keep, r, settle_gather)
     sums_out[...] = jnp.sum(total, axis=0, keepdims=True)
-    spread = jnp.dot(unplace[...], total.astype(BF), preferred_element_type=F32).astype(BF)
+    spread = jnp.dot(unplace[...], padded(total).astype(BF), preferred_element_type=F32).astype(BF)
     rsend[...] = spread.reshape(8, 4, 16, HD)
     finish()
 
@@ -612,7 +623,7 @@
 VMEM = pl.BlockSpec(memory_space=pltpu.VMEM)
 ANY = pl.BlockSpec(memory_space=pl.ANY)
 DMA = pltpu.SemaphoreType.DMA
-COMMON = 256
+COMMON = 272
 
 PROJECT_SCRATCH = [
     ("q", pltpu.VMEM((32, 1024), BF)),
@@ -659,11 +670,11 @@
         ("part", pltpu.VMEM((4, rows, 512), F32)),
         ("y1s", pltpu.VMEM((4, 2, rows, HD), BF)),
         ("y1r", pltpu.VMEM((4, 2, rows, HD), BF)),
-        ("y2s", pltpu.VMEM((4, 2, rows // 2, HD), BF)),
-        ("y2r", pltpu.VMEM((4, 2, rows // 2, HD), BF)),
+        ("y2s", pltpu.VMEM((4, 2, upper_half(rows), HD), BF)),
+        ("y2r", pltpu.VMEM((4, 2, upper_half(rows), HD), BF)),
         ("zsend", pltpu.VMEM((3, rows, HD), BF)),
         ("zrecv", pltpu.VMEM((3, rows, HD), BF)),
-        ("unplace", pltpu.VMEM((512, rows), BF)),
+        ("unplace", pltpu.VMEM((512, -(-rows // 128) * 128), BF)),
         ("rsend", pltpu.VMEM((8, 4, 16, HD), BF)),
         ("rbuf", pltpu.VMEM((4, 8, 16, HD), BF)),
         ("final", pltpu.VMEM((4, 8, 32, HD), BF)),

time: 90.6 us -> 91.6 us (1.011)
  Pallas kernels: 87.8 us -> 88.8 us
    pallas_call x1, Pallas kernels: 87.8 us -> 88.8 us  [call(): pl.pallas_call(kernel, name=name, out_shape=tuple((shape for _, shape, _...]
where the time goes in v4:
time: 91.6 us; the launch traced here: 91.5 us
  Pallas kernels  88.8 us (97%)
  between operations  1.28 us (1%)
  local copies, waits for them, and re-layouts  1.22 us (1%)
    pallas_call x1, Pallas kernels, call(): pl.pallas_call(kernel, name=name, out_shape=tuple((shape for _, shape, _...  88.8 us

profile of v4, /device:TPU:1, one launch (start us, length us, event | category | flops | bytes accessed | tf_op | source)
XLA Modules:
  0.0 91.5 jit_solution(3249725837736458076)
XLA Ops:
  0.6 0.0 copy-start
  0.6 88.8 %layer.1 = (bf16[32,4096]{1,0:T(8,128)(2,1)S(1)}, f32[1,128]{1,0:T(1,128)S(1)}, bf16[512,128]{1,0:T(8,128)(2,1)S(1)}, f32[256,128]{1,0:T(8,128)S(1)}, bf16[64,12...) custom-call(bf16[32,1024]{1,0:T(8,128)(2,1)} %refs_0_.1, bf16[32,128,128]{2,1,0:T(8,128)(2,1)} %refs_1_.1, ...), custom_call_target="tpu_custom_call" | custom-call | tf_op jit(solution)/shard_map/layer/pallas_call | solution.py:713
  90.1 0.0 copy-done
  90.1 0.2 conditional.1
  90.3 0.7 copy.23
  91.0 0.5 copy.24
Async XLA Ops:
  0.6 89.5 %copy-start = (f32[128]{0:T(128)S(1)}, f32[128]{0:T(128)}, u32[]{:S(2)}) copy-start(f32[128]{0:T(128)} %param.20) | copy-start | bytes 1540
